TPU v7x, 32 devices: a whole 2x2x4 slice. The times are simulated.
32 devices in a mesh: outer: 4 (over y, x), inner: 8 (over z, core).
Axes of the slice: x: 2, y: 2, z: 4, core: 2. Of those that a mesh axis runs over, the one named last changes fastest.
Arguments:
- query_rows: bfloat16 [4096, 4096], P(('outer', 'inner')), may hold values from -6 to 6
- key_rows: bfloat16 [4096, 4096], P(('outer', 'inner')), may hold values from -6 to 6
- value_rows: bfloat16 [4096, 4096], P(('outer', 'inner')), may hold values from -6 to 6
- out_grad: bfloat16 [4096, 4096], P(('outer', 'inner')), may hold values from -6 to 6
- filter_rows: bfloat16 [4096, 4096], P(('outer', 'inner')), may hold values from -0.09375 to 0.09375
- skip_gain: float32 [4096], replicated, may hold values from -1 to 1
Outputs:
- layer_out: bfloat16 [4096, 4096], P(('outer', 'inner'))
- query_grad: bfloat16 [4096, 4096], P(('outer', 'inner'))
- key_grad: bfloat16 [4096, 4096], P(('outer', 'inner'))
- value_grad: bfloat16 [4096, 4096], P(('outer', 'inner'))
- filter_grad: bfloat16 [4096, 4096], P(('outer', 'inner'))
- skip_grad: float32 [4096], replicated
All inputs are finite; a program needn't handle non-finite values.
Results may differ from a plain program's by a relative error of at most 0.0085.
Values may be sent and summed in bfloat16 or wider, within the bound.
No kernel may reach another device: no remote copies, remote signals or barrier semaphores. Data moves between devices by JAX's collectives and lax.ppermute only.
A program may use at most 128 MiB of HBM per device.

v0:
```python
import math

import jax
import jax.numpy as jnp
from jax import lax
from jax.sharding import PartitionSpec as P

TWO_PI = 2.0 * math.pi


def rounded_trig(phase, modulus):
    angle = (phase % modulus).astype(jnp.float32) * (TWO_PI / modulus)
    return (jnp.cos(angle).astype(jnp.bfloat16), jnp.sin(angle).astype(jnp.bfloat16))


def regroup_blocks(blocks):
    return lax.all_to_all(blocks, ("outer", "inner"), split_axis=0, concat_axis=0, tiled=True)


def body(query_rows, key_rows, value_rows, out_grad, filter_rows, skip_gain):
    devices = lax.axis_size(("outer", "inner"))
    position = lax.axis_index(("outer", "inner"))
    tokens_here = query_rows.shape[0]
    channels = query_rows.shape[1]
    piece_rows = tokens_here // devices
    length = tokens_here * devices
    points = 2 * length
    radix_count = 2 * devices
    factor = 1.0 / math.sqrt(length)
    product = (key_rows.astype(jnp.float32) * value_rows.astype(jnp.float32)).astype(jnp.bfloat16)
    gate_grad = out_grad.astype(jnp.float32) * query_rows.astype(jnp.float32)
    signals = jnp.stack([product, gate_grad.astype(jnp.bfloat16), filter_rows], axis=1)
    columns = regroup_blocks(signals.reshape(devices, piece_rows, 3, channels))
    anchor = jnp.arange(devices, dtype=jnp.int32)
    halves = jnp.arange(2, dtype=jnp.int32)
    local_steps = jnp.arange(piece_rows, dtype=jnp.int32)
    step_index = jnp.arange(tokens_here, dtype=jnp.int32)
    sample = position * piece_rows + local_steps
    section_one = []
    for half in range(2):
        freq_one = half * devices + anchor
        phase = (
            anchor[None, None, :] * freq_one[None, :, None] * tokens_here
            + sample[:, None, None] * freq_one[None, :, None]
        )
        one_cos, one_sin = rounded_trig(phase, points)
        table_one = jnp.stack([one_cos, -one_sin], axis=2).reshape(piece_rows, 2 * devices, devices)
        result = jnp.einsum(
            "skr,rsbc->ksbc", table_one, columns, preferred_element_type=jnp.float32
        )
        section_one.append(result.astype(jnp.bfloat16).reshape(devices, 2, piece_rows, 3, channels))
    section_one = regroup_blocks(jnp.stack(section_one, axis=2))
    full_sample = anchor[:, None] * piece_rows + local_steps[None, :]
    step_cos, step_sin = rounded_trig(
        full_sample[:, :, None] * step_index[None, None, :], tokens_here
    )
    real_col = jnp.stack([step_cos, step_sin])
    imag_col = jnp.stack([-step_sin, step_cos])
    table_two = jnp.stack([real_col, imag_col], axis=3)
    section_three = []
    for half in range(2):
        spectra = jnp.einsum(
            "oisbc,iosjk->jkbc",
            section_one[:, :, half],
            table_two,
            preferred_element_type=jnp.float32,
        )
        spec_real, spec_imag = (spectra[0], spectra[1])
        value_real, gate_real, filter_real = (spec_real[:, 0], spec_real[:, 1], spec_real[:, 2])
        value_imag, gate_imag, filter_imag = (spec_imag[:, 0], spec_imag[:, 1], spec_imag[:, 2])
        forward_real = value_real * filter_real - value_imag * filter_imag
        forward_imag = value_real * filter_imag + value_imag * filter_real
        backward_real = filter_real * gate_real + filter_imag * gate_imag
        backward_imag = filter_real * gate_imag - filter_imag * gate_real
        lag_real = (value_real * gate_real + value_imag * gate_imag) * factor
        lag_imag = (value_real * gate_imag - value_imag * gate_real) * factor
        products = jnp.stack(
            [
                jnp.stack([forward_real, backward_real, lag_real], axis=1),
                jnp.stack([forward_imag, backward_imag, lag_imag], axis=1),
            ]
        ).astype(jnp.bfloat16)
        freq_held = half * devices + position
        phase_three = (
            step_index[None, :] * step_index[:, None] * radix_count
            + step_index[None, :] * freq_held
        )
        three_cos, three_sin = rounded_trig(phase_three, points)
        real_row = jnp.stack([three_cos, -three_sin])
        imag_row = jnp.stack([three_sin, three_cos])
        table_three = jnp.stack([real_row, imag_row], axis=2)
        result = jnp.einsum(
            "ikbc,ikjs->sjbc", products, table_three, preferred_element_type=jnp.float32
        )
        section_three.append(result.astype(jnp.bfloat16))
    section_three = jnp.stack(section_three, axis=2).reshape(devices, piece_rows, 2, 2, 3, channels)
    rows_back = regroup_blocks(section_three)
    freq_last = halves[:, None] * devices + anchor[None, :]
    last_cos, last_sin = rounded_trig(anchor[None, None, :] * freq_last[:, :, None], radix_count)
    table_four = jnp.stack([last_cos, -last_sin])
    restored = (
        jnp.einsum("opjhbc,jhor->rpbc", rows_back, table_four, preferred_element_type=jnp.float32)
        / points
    )
    home_rows = regroup_blocks(restored.astype(jnp.bfloat16)).reshape(tokens_here, 3, channels)
    convolved = home_rows[:, 0].astype(jnp.float32)
    correlated = home_rows[:, 1].astype(jnp.float32)
    filter_grad = home_rows[:, 2]
    product_full = product.astype(jnp.float32)
    mixing = convolved + skip_gain[None, :] * product_full
    layer_out = (query_rows.astype(jnp.float32) * mixing).astype(jnp.bfloat16)
    query_grad = (out_grad.astype(jnp.float32) * mixing).astype(jnp.bfloat16)
    carried = correlated + skip_gain[None, :] * gate_grad
    key_grad = (carried * value_rows.astype(jnp.float32)).astype(jnp.bfloat16)
    value_grad = (carried * key_rows.astype(jnp.float32)).astype(jnp.bfloat16)
    skip_part = jnp.sum(gate_grad * product_full, axis=0)
    skip_sum = lax.psum(skip_part, ("outer", "inner"))
    return (layer_out, query_grad, key_grad, value_grad, filter_grad, skip_sum * factor)


def solution(mesh):
    return jax.shard_map(
        body,
        mesh=mesh,
        in_specs=(
            P(("outer", "inner"), None),
            P(("outer", "inner"), None),
            P(("outer", "inner"), None),
            P(("outer", "inner"), None),
            P(("outer", "inner"), None),
            P(),
        ),
        out_specs=(
            P(("outer", "inner"), None),
            P(("outer", "inner"), None),
            P(("outer", "inner"), None),
            P(("outer", "inner"), None),
            P(("outer", "inner"), None),
            P(),
        ),
        check_vma=False,
    )
```

profile of v0, /device:TPU:0, one launch (start us, length us, event | category | flops | bytes accessed | tf_op | source)
XLA Modules:
  0.0 986.2 jit_solution(2784821486954120887)
XLA Ops:
  0.6 3.0 fusion.25
  3.6 0.4 stack.159
  4.1 1.2 stack.160
  5.3 1.5 stack.161
  6.8 3.9 pad_maximum_fusion.4
  10.6 3.1 copy.62
  13.7 7.3 all-to-all-start
  21.2 0.6 cosine_convert_fusion.1
  21.8 0.6 fusion.52
  22.5 71.1 %all-to-all-done = bf16[32,4,3,4096]{3,1,2,0:T(4,128)(2,1)S(1)} async-done(((bf16[32,4,3,4096]{3,1,2,0:T(4,128)(2,1)}), bf16[32,4,3,4096]{3,1,2,0:T(4,128)(2,1)S(1)}, u32[]{:S(2)}, u32[]{:S(2)}) %all-to-all-start) | async-done | bytes 3145760 | tf_op jit(solution)/shard_map/all_to_all | solution.py:17
  93.6 7.5 fusion.7
  101.1 11.1 %stack_reshape.6 = bf16[32,2,1,4,3,4096]{5,1,0,4,3,2:T(2,128)(2,1)} reshape(bf16[64,4,3,4096]{3,0,2,1:T(8,128)(2,1)} %fusion.7) | data formatting | bytes 12582912 | tf_op jit(solution)/shard_map/stack;reshape | solution.py:52
  112.3 30.4 %copy.69 = bf16[32,2,1,4,3,4096]{5,3,1,4,2,0:T(4,128)(2,1)} copy(bf16[32,2,1,4,3,4096]{5,1,0,4,3,2:T(2,128)(2,1)} %stack_reshape.6) | data formatting | bytes 12582912 | tf_op jit(solution)/shard_map/stack;reshape | solution.py:52
  142.7 7.5 fusion.8
  150.2 11.0 %stack_reshape.7 = bf16[32,2,1,4,3,4096]{5,1,0,4,3,2:T(2,128)(2,1)} reshape(bf16[64,4,3,4096]{3,0,2,1:T(8,128)(2,1)} %fusion.8) | data formatting | bytes 12582912 | tf_op jit(solution)/shard_map/stack;reshape | solution.py:52
  161.2 18.6 %copy.70 = bf16[32,2,1,4,3,4096]{5,3,1,4,2,0:T(4,128)(2,1)} copy(bf16[32,2,1,4,3,4096]{5,1,0,4,3,2:T(2,128)(2,1)} %stack_reshape.7) | data formatting | bytes 12582912 | tf_op jit(solution)/shard_map/stack;reshape | solution.py:52
  179.9 10.9 %pad_maximum_fusion = bf16[32,2,2,4,3,4096]{5,3,1,4,2,0:T(4,128)(2,1)} fusion(bf16[32,2,1,4,3,4096]{5,3,1,4,2,0:T(4,128)(2,1)} %copy.70, bf16[32,2,1,4,3,4096]{5,3,1,4,2,0:T(4,128)(2,1)S(1)} %bitcast.141), kind=kLoop, calls=%fused_computation | loop fusion | flops 6291456 | bytes 25165824 | tf_op jit(solution)/shard_map/stack | solution.py:52
  190.8 3.8 all-to-all-start.1
  195.6 0.3 sine_convert_fusion.4
  196.3 0.3 sine_convert_fusion
  196.7 272.6 %all-to-all-done.1 = bf16[32,2,2,4,3,4096]{5,3,1,4,2,0:T(4,128)(2,1)} async-done(((bf16[32,2,2,4,3,4096]{5,3,1,4,2,0:T(4,128)(2,1)}), bf16[32,2,2,4,3,4096]{5,3,1,4,2,0:T(4,128)(2,1)}, u32[]{:S(2)}, u32[]{:S(2)}) %all-to-all-start.1) | async-done | bytes 12582944 | tf_op jit(solution)/shard_map/all_to_all | solution.py:17
  469.3 11.2 %fusion.69 = (bf16[32,2,1,4,3,4096]{5,3,1,4,2,0:T(4,128)(2,1)S(1)}, bf16[32,2,1,4,3,4096]{5,3,1,4,2,0:T(4,128)(2,1)}) fusion(bf16[32,2,2,4,3,4096]{5,3,1,4,2,0:T(4,128)(2,1)} %all-to-all-done.1), kind=kLoop, calls=%fused_computation.168 | loop fusion | bytes 25165824 | tf_op jit(solution)/shard_map/slice | solution.py:64
  480.5 9.0 convolution_bitcast_fusion.1
  489.5 8.4 slice_bitcast_fusion.3
  497.9 5.6 add_convert_fusion.3
  503.5 3.1 subtract_convert_fusion.3
  506.6 9.0 convolution_bitcast_fusion
  515.6 8.4 slice_bitcast_fusion.1
  524.0 4.3 add_convert_fusion.1
  528.3 0.4 copy-done.1
  528.7 2.4 subtract_convert_fusion.1
  531.4 0.8 copy-done.3
  533.2 2.0 fusion.9
  535.3 12.8 %copy.95 = bf16[128,2,3,4096]{3,1,2,0:T(2,128)(2,1)S(1)} copy(bf16[128,2,3,4096]{3,0,2,1:T(8,128)(2,1)S(1)} %fusion.9) | data formatting | bytes 12582912 | tf_op jit(solution)/shard_map/stack | solution.py:96
  548.9 2.0 fusion.12
  550.9 12.8 %copy.96 = bf16[128,2,3,4096]{3,1,2,0:T(2,128)(2,1)S(1)} copy(bf16[128,2,3,4096]{3,0,2,1:T(8,128)(2,1)S(1)} %fusion.12) | data formatting | bytes 12582912 | tf_op jit(solution)/shard_map/stack | solution.py:96
  563.7 18.0 %pad_maximum_fusion.1 = bf16[32,4,2,2,3,4096]{5,2,3,4,1,0:T(2,128)(2,1)} fusion(bf16[32,4,2,1,3,4096]{5,2,3,4,1,0:T(2,128)(2,1)S(1)} %bitcast.142, bf16[32,4,2,1,3,4096]{5,2,3,4,1,0:T(2,128)(2,1)S(1)} %bitcast.139), kind=kLoop, calls=%fused_computation.1 | loop fusion | flops 6291456 | bytes 25165824 | tf_op jit(solution)/shard_map/stack | solution.py:96
  581.7 4.0 all-to-all-start.2
  586.1 274.4 %all-to-all-done.2 = bf16[32,4,2,2,3,4096]{5,2,3,4,1,0:T(2,128)(2,1)} async-done(((bf16[32,4,2,2,3,4096]{5,2,3,4,1,0:T(2,128)(2,1)}), bf16[32,4,2,2,3,4096]{5,2,3,4,1,0:T(2,128)(2,1)}, u32[]{:S(2)}, u32[]{:S(2)}) %all-to-all-start.2) | async-done | bytes 12582944 | tf_op jit(solution)/shard_map/all_to_all | solution.py:17
  860.5 12.1 %fusion.2 = bf16[32,4,3,4096]{3,0,2,1:T(8,128)(2,1)S(1)} fusion(bf16[32,4,2,2,3,4096]{5,2,3,4,1,0:T(2,128)(2,1)} %all-to-all-done.2, bf16[1,2,32,32]{2,3,0,1:T(8,128)(2,1)S(1)} %fusion.59, bf16[1,2,32,32]{2,3,0,1:T(8,128)(2,1)S(1)} %cosine_convert_fusion.5), kind=kOutput, calls=%fused_computation.19 | convolution fusion | flops 405815296 | bytes 15736832 | tf_op jit(solution)/shard_map/opjhbc,jhor->rpbc/dot_general | solution.py:102
  872.6 4.1 copy.78
  876.7 2.8 all-to-all-start.3
  879.5 91.6 %psum.7 = f32[4096]{0:T(1024)S(1)} all-reduce(f32[4096]{0:T(1024)S(1)} %get-tuple-element.6), channel_id=1, replica_groups=mesh['outer'=4,'inner'=8] {'outer','inner'}, use_global_device_ids=true, to_apply=%region_1.2 | all-reduce | flops 4096 | bytes 32768 | tf_op jit(solution)/shard_map/psum | solution.py:117
  971.1 0.6 broadcast_multiply_fusion
  971.7 3.1 copy.79
  974.8 3.8 reshape.711
  978.6 1.0 slice_bitcast_fusion.4
  979.6 6.2 fusion.20
  (61 shorter events, 4.1 us)
Async XLA Ops:
  3.6 3.1 copy-start.2
  13.7 79.9 %all-to-all-start = ((bf16[32,4,3,4096]{3,1,2,0:T(4,128)(2,1)}), bf16[32,4,3,4096]{3,1,2,0:T(4,128)(2,1)S(1)}, u32[]{:S(2)}, u32[]{:S(2)}) async-start(bf16[32,4,3,4096]{3,1,2,0:T(4,128)(2,1)} %copy.62), calls=%async_computation | async-start | bytes 6291456 | tf_op jit(solution)/shard_map/all_to_all | solution.py:17
  150.2 29.7 %slice-start = ((s8[6291456]{0:T(1024)(128)(4,1)}), s8[2097152]{0:T(1024)(128)(4,1)S(1)}, s32[]{:S(2)}) async-start(s8[6291456]{0:T(1024)(128)(4,1)} %bitcast.140), calls=%async_computation.4 | async-start | bytes 4194304
  161.2 18.6 %slice-start.1 = ((s8[6291456]{0:T(1024)(128)(4,1)}), s8[4194304]{0:T(1024)(128)(4,1)S(1)}, s32[]{:S(2)}) async-start(s8[6291456]{0:T(1024)(128)(4,1)} %bitcast.140), calls=%async_computation.5 | async-start | bytes 8388608
  190.8 278.6 %all-to-all-start.1 = ((bf16[32,2,2,4,3,4096]{5,3,1,4,2,0:T(4,128)(2,1)}), bf16[32,2,2,4,3,4096]{5,3,1,4,2,0:T(4,128)(2,1)}, u32[]{:S(2)}, u32[]{:S(2)}) async-start(bf16[32,2,2,4,3,4096]{5,3,1,4,2,0:T(4,128)(2,1)} %pad_maximum_fusion), calls=%async_computation.1 | async-start | bytes 25165824 | tf_op jit(solution)/shard_map/all_to_all | solution.py:17
  497.9 5.6 copy-start
  497.9 8.7 slice-start.2
  503.5 3.1 slice-start.3
  524.0 4.7 copy-start.1
  528.7 2.4 copy-start.4
  528.7 2.4 copy-start.7
  528.7 2.4 copy-start.8
  531.0 1.2 copy-start.3
  531.0 1.5 copy-start.5
  531.1 1.8 copy-start.6
  535.3 12.9 %copy-start.9 = (bf16[128,1,4096]{2,0,1:T(8,128)(2,1)S(1)}, bf16[128,1,4096]{2,0,1:T(8,128)(2,1)}, u32[]{:S(2)}) copy-start(bf16[128,1,4096]{2,0,1:T(8,128)(2,1)} %get-tuple-element.18) | copy-start | bytes 3145732
  535.3 12.9 %copy-start.10 = (bf16[128,1,4096]{2,0,1:T(8,128)(2,1)S(1)}, bf16[128,1,4096]{2,0,1:T(8,128)(2,1)}, u32[]{:S(2)}) copy-start(bf16[128,1,4096]{2,0,1:T(8,128)(2,1)} %get-tuple-element.19) | copy-start | bytes 3145732
  581.7 278.8 %all-to-all-start.2 = ((bf16[32,4,2,2,3,4096]{5,2,3,4,1,0:T(2,128)(2,1)}), bf16[32,4,2,2,3,4096]{5,2,3,4,1,0:T(2,128)(2,1)}, u32[]{:S(2)}, u32[]{:S(2)}) async-start(bf16[32,4,2,2,3,4096]{5,2,3,4,1,0:T(2,128)(2,1)} %pad_maximum_fusion.1), calls=%async_computation.2 | async-start | bytes 25165824 | tf_op jit(solution)/shard_map/all_to_all | solution.py:17
  876.7 95.0 %all-to-all-start.3 = ((bf16[32,4,3,4096]{3,1,2,0:T(4,128)(2,1)}), bf16[32,4,3,4096]{3,1,2,0:T(4,128)(2,1)S(1)}, u32[]{:S(2)}, u32[]{:S(2)}) async-start(bf16[32,4,3,4096]{3,1,2,0:T(4,128)(2,1)} %copy.78), calls=%async_computation.3 | async-start | bytes 6291456 | tf_op jit(solution)/shard_map/all_to_all | solution.py:17
  974.8 4.8 copy-start.11
where the time goes:
time: 995 us; the launch traced here: 986 us
  waiting for transfers between devices  618 us (62%)
  local copies, waits for them, and re-layouts  145 us (15%)
  blocking collectives  91.6 us (9%)
  other arithmetic  62.9 us (6%)
  matrix products  49.2 us (5%)
  starting transfers between devices  17.8 us (2%)
    all_to_all x4, waiting for transfers between devices, regroup_blocks(): lax.all_to_all(blocks, ('outer', 'inner'), split_axis=0, concat_axis=0, t...  618 us
    psum x1, blocking collectives, body(): skip_sum = lax.psum(skip_part, ('outer', 'inner'))  91.6 us
    another operation x4, local copies, waits for them, and re-layouts, body(): section_one = regroup_blocks(jnp.stack(section_one, axis=2))  71.2 us
    another operation x2, local copies, waits for them, and re-layouts, body(): jnp.stack(section_three, axis=2)  25.7 us
  transfers between devices with their start and end apart: 4, of which 3 were waited for; matrix products, arithmetic and copies ran while one was open for 0% of the time, Pallas kernels for 0%

commit v1 on v0

--- a/solution.py
+++ b/solution.py
@@ -1,11 +1,273 @@
+import functools
 import math
 
 import jax
 import jax.numpy as jnp
+import ml_dtypes
+import numpy as np
 from jax import lax
+from jax.experimental import pallas as pl
+from jax.experimental.pallas import tpu as pltpu
 from jax.sharding import PartitionSpec as P
 
 TWO_PI = 2.0 * math.pi
+AXES = ("outer", "inner")
+LANES = 128
+SUBLANES = 8
+BF16 = jnp.bfloat16
+F32 = jnp.float32
+
+
+def table_trig(phase, modulus):
+    angle = (phase % modulus).astype(np.float32) * np.float32(TWO_PI / modulus)
+    return tuple(
+        part.astype(ml_dtypes.bfloat16).astype(np.float32) for part in (np.cos(angle), np.sin(angle))
+    )
+
+
+def make_tables(rows, steps):
+    planes = rows + 1
+    points = 2 * rows * steps
+    row = np.arange(rows)
+    plane = np.arange(planes)
+    step = np.arange(steps)
+    eye = np.eye(SUBLANES, dtype=np.float32)
+    phase = row[None, None, :] * plane[None, :, None] * steps + step[:, None, None] * plane[None, :, None]
+    cos, sin = table_trig(phase, points)
+    first = np.stack([cos, -sin], axis=1).reshape(steps // SUBLANES, SUBLANES, 2, planes, rows)
+    first = np.einsum("bipkr,ij->bpkirj", first, eye)
+    first = first.reshape(steps // SUBLANES, 2 * planes * SUBLANES, rows * SUBLANES)
+    cos, sin = table_trig(step[:, None] * step[None, :], steps)
+    second = np.block([[cos, sin], [-sin, cos]])
+    phase = step[None, :, None] * step[None, None, :] * (2 * rows) + step[None, :, None] * plane[:, None, None]
+    cos, sin = table_trig(phase, points)
+    third = np.concatenate(
+        [np.concatenate([cos, -sin], axis=2), np.concatenate([sin, cos], axis=2)], axis=1
+    )
+    cos, sin = table_trig(row[:, None] * plane[None, :], 2 * rows)
+    weight = np.where((plane == 0) | (plane == rows), 1.0, 2.0).astype(np.float32)
+    last = np.stack([cos * weight, -sin * weight], axis=1)
+    last = np.einsum("rpk,ij->ripkj", last, eye).reshape(rows * SUBLANES, 2 * planes * SUBLANES)
+    return tuple(table.astype(ml_dtypes.bfloat16) for table in (first, second, third, last))
+
+
+def dot(a, b):
+    return jnp.dot(a, b, preferred_element_type=F32)
+
+
+def pack_kernel(filter_ref, key_ref, value_ref, out_ref):
+    blocks = out_ref.shape[0]
+    tokens = filter_ref.shape[0]
+    for j in range(blocks):
+        cols = pl.ds(j * LANES, LANES)
+        out_ref[j, :tokens, :] = filter_ref[:, cols]
+        product = key_ref[:, cols].astype(F32) * value_ref[:, cols].astype(F32)
+        out_ref[j, tokens:, :] = product.astype(BF16)
+
+
+def gate_kernel(query_ref, grad_ref, key_ref, value_ref, out_ref, skip_ref):
+    blocks = out_ref.shape[0]
+    for j in range(blocks):
+        cols = pl.ds(j * LANES, LANES)
+        gate = grad_ref[:, cols].astype(F32) * query_ref[:, cols].astype(F32)
+        product = (key_ref[:, cols].astype(F32) * value_ref[:, cols].astype(F32)).astype(BF16).astype(F32)
+        out_ref[j] = gate.astype(BF16)
+        skip_ref[:, cols] = jnp.sum(gate * product, axis=0, keepdims=True)
+
+
+def spectra_of(read_pair, first_ref, second_ref, section, store):
+    planes = section.shape[0]
+    steps = section.shape[1] // 2
+    width = section.shape[2]
+
+    def one(b, _):
+        pair = read_pair(b)
+        for half in range(2):
+            block = pair[:, half * SUBLANES : (half + 1) * SUBLANES, :]
+            flat = block.reshape(-1, width).astype(BF16)
+            result = dot(first_ref[2 * b + half], flat).reshape(2, planes, SUBLANES, width)
+            at = pl.multiple_of((2 * b + half) * SUBLANES, SUBLANES)
+            section[:, pl.ds(at, SUBLANES), :] = result[0]
+            section[:, pl.ds(steps + at, SUBLANES), :] = result[1]
+        return 0
+
+    lax.fori_loop(0, steps // (2 * SUBLANES), one, 0)
+
+    def two(k, _):
+        store(k, dot(second_ref[...], section[k].astype(BF16)))
+        return 0
+
+    lax.fori_loop(0, planes, two, 0)
+
+
+def inverse_of(product_at, third_ref, last_ref, section, scale, write_pair):
+    planes = section.shape[0]
+    steps = section.shape[1] // 2
+    width = section.shape[2]
+
+    def three(k, _):
+        section[k] = dot(third_ref[k], product_at(k))
+        return 0
+
+    lax.fori_loop(0, planes, three, 0)
+
+    def four(b, _):
+        halves = []
+        for half in range(2):
+            at = pl.multiple_of((2 * b + half) * SUBLANES, SUBLANES)
+            real = section[:, pl.ds(at, SUBLANES), :].reshape(-1, width)
+            imag = section[:, pl.ds(steps + at, SUBLANES), :].reshape(-1, width)
+            flat = jnp.concatenate([real, imag], axis=0).astype(BF16)
+            halves.append((dot(last_ref[...], flat) * scale).reshape(-1, SUBLANES, width))
+        write_pair(b, jnp.concatenate(halves, axis=1))
+        return 0
+
+    lax.fori_loop(0, steps // (2 * SUBLANES), four, 0)
+
+
+def pair_rows(b):
+    return pl.ds(pl.multiple_of(b * 2 * SUBLANES, 2 * SUBLANES), 2 * SUBLANES)
+
+
+def forward_kernel(steps, scale, packed_ref, first_ref, second_ref, third_ref, last_ref, out_ref, spectra_ref, section, narrow):
+    def read_pair(b):
+        return jnp.concatenate(
+            [
+                packed_ref[:, pair_rows(b), :].astype(F32),
+                packed_ref[:, pair_rows(b + steps // (2 * SUBLANES)), :].astype(F32),
+            ],
+            axis=2,
+        )
+
+    def store(k, plane):
+        spectra_ref[k] = plane
+
+    spectra_of(read_pair, first_ref, second_ref, section, store)
+
+    def product_at(k):
+        filt = spectra_ref[k, :, :LANES]
+        value = spectra_ref[k, :, LANES:]
+        fr, fi, vr, vi = filt[:steps], filt[steps:], value[:steps], value[steps:]
+        return jnp.concatenate([vr * fr - vi * fi, vr * fi + vi * fr], axis=0).astype(BF16)
+
+    def write_pair(b, rows):
+        out_ref[:, pair_rows(b), :] = rows.astype(BF16)
+
+    inverse_of(product_at, third_ref, last_ref, narrow, scale, write_pair)
+
+
+def backward_kernel(steps, scale, factor, gate_ref, spectra_ref, first_ref, second_ref, third_ref, last_ref, out_ref, section, gate_spectrum, wide):
+    def read_pair(b):
+        return gate_ref[:, pair_rows(b), :].astype(F32)
+
+    def store(k, plane):
+        gate_spectrum[k] = plane
+
+    spectra_of(read_pair, first_ref, second_ref, section, store)
+
+    def product_at(k):
+        both = spectra_ref[k]
+        gate = gate_spectrum[k]
+        gate = jnp.concatenate([gate, gate], axis=1)
+        br, bi, gr, gi = both[:steps], both[steps:], gate[:steps], gate[steps:]
+        full = jnp.concatenate([br * gr + bi * gi, br * gi - bi * gr], axis=0)
+        return jnp.concatenate([full[:, :LANES], full[:, LANES:] * factor], axis=1).astype(BF16)
+
+    def write_pair(b, rows):
+        out_ref[:, pair_rows(b), :] = rows[:, :, :LANES].astype(BF16)
+        out_ref[:, pair_rows(b + steps // (2 * SUBLANES)), :] = rows[:, :, LANES:].astype(BF16)
+
+    inverse_of(product_at, third_ref, last_ref, wide, scale, write_pair)
+
+
+def mixing_kernel(conv_ref, query_ref, grad_ref, key_ref, value_ref, gain_ref, layer_ref, query_grad_ref):
+    for j in range(conv_ref.shape[0]):
+        cols = pl.ds(j * LANES, LANES)
+        product = (key_ref[:, cols].astype(F32) * value_ref[:, cols].astype(F32)).astype(BF16).astype(F32)
+        mixing = conv_ref[j].astype(F32) + gain_ref[:, cols] * product
+        layer_ref[:, cols] = (query_ref[:, cols].astype(F32) * mixing).astype(BF16)
+        query_grad_ref[:, cols] = (grad_ref[:, cols].astype(F32) * mixing).astype(BF16)
+
+
+def carried_kernel(back_ref, query_ref, grad_ref, key_ref, value_ref, gain_ref, key_grad_ref, value_grad_ref, filter_grad_ref):
+    tokens = query_ref.shape[0]
+    for j in range(back_ref.shape[0]):
+        cols = pl.ds(j * LANES, LANES)
+        gate = grad_ref[:, cols].astype(F32) * query_ref[:, cols].astype(F32)
+        carried = back_ref[j, :tokens, :].astype(F32) + gain_ref[:, cols] * gate
+        key_grad_ref[:, cols] = (carried * value_ref[:, cols].astype(F32)).astype(BF16)
+        value_grad_ref[:, cols] = (carried * key_ref[:, cols].astype(F32)).astype(BF16)
+        filter_grad_ref[:, cols] = back_ref[j, tokens:, :]
+
+
+def exchange(blocks):
+    return lax.all_to_all(blocks, AXES, split_axis=0, concat_axis=0, tiled=True)
+
+
+def limit(mib):
+    return pltpu.CompilerParams(vmem_limit_bytes=mib * 1024 * 1024)
+
+
+def channel_body(query_rows, key_rows, value_rows, out_grad, filter_rows, skip_gain):
+    devices = lax.axis_size(AXES)
+    tokens, channels = query_rows.shape
+    length = tokens * devices
+    factor = 1.0 / math.sqrt(length)
+    scale = 1.0 / (2 * length)
+    planes = devices + 1
+    first, second, third, last = (jnp.asarray(t) for t in make_tables(devices, tokens))
+    group = math.gcd(devices, 8)
+    grid = (devices // group,)
+    rows_spec = pl.BlockSpec((tokens, group * LANES), lambda i: (0, i))
+    vector_spec = pl.BlockSpec((1, group * LANES), lambda i: (0, i))
+    single_spec = pl.BlockSpec((group, tokens, LANES), lambda i: (i, 0, 0))
+    double_spec = pl.BlockSpec((group, 2 * tokens, LANES), lambda i: (i, 0, 0))
+    rows_shape = jax.ShapeDtypeStruct((tokens, channels), BF16)
+    single_shape = jax.ShapeDtypeStruct((devices, tokens, LANES), BF16)
+    double_shape = jax.ShapeDtypeStruct((devices, 2 * tokens, LANES), BF16)
+
+    packed = pl.pallas_call(
+        pack_kernel, grid=grid, in_specs=[rows_spec] * 3, out_specs=double_spec, out_shape=double_shape,
+    )(filter_rows, key_rows, value_rows)
+    packed = exchange(packed)
+    gate, skip_part = pl.pallas_call(
+        gate_kernel, grid=grid, in_specs=[rows_spec] * 4, out_specs=[single_spec, vector_spec],
+        out_shape=[single_shape, jax.ShapeDtypeStruct((1, channels), F32)],
+    )(query_rows, out_grad, key_rows, value_rows)
+    skip_parts = lax.all_gather(skip_part, AXES, axis=0, tiled=True)
+    gate = exchange(gate)
+    convolved, spectra = pl.pallas_call(
+        functools.partial(forward_kernel, tokens, scale),
+        out_shape=[single_shape, jax.ShapeDtypeStruct((planes, 2 * tokens, 2 * LANES), F32)],
+        scratch_shapes=[
+            pltpu.VMEM((planes, 2 * tokens, 2 * LANES), F32),
+            pltpu.VMEM((planes, 2 * tokens, LANES), F32),
+        ],
+        compiler_params=limit(48),
+    )(packed, first, second, third, last)
+    convolved = exchange(convolved)
+    back = pl.pallas_call(
+        functools.partial(backward_kernel, tokens, scale, factor),
+        out_shape=double_shape,
+        scratch_shapes=[
+            pltpu.VMEM((planes, 2 * tokens, LANES), F32),
+            pltpu.VMEM((planes, 2 * tokens, LANES), F32),
+            pltpu.VMEM((planes, 2 * tokens, 2 * LANES), F32),
+        ],
+        compiler_params=limit(48),
+    )(gate, spectra, first, second, third, last)
+    back = exchange(back)
+    gain = skip_gain[None, :]
+    layer_out, query_grad = pl.pallas_call(
+        mixing_kernel, grid=grid, in_specs=[single_spec] + [rows_spec] * 4 + [vector_spec],
+        out_specs=[rows_spec] * 2, out_shape=[rows_shape] * 2,
+    )(convolved, query_rows, out_grad, key_rows, value_rows, gain)
+    key_grad, value_grad, filter_grad = pl.pallas_call(
+        carried_kernel, grid=grid, in_specs=[double_spec] + [rows_spec] * 4 + [vector_spec],
+        out_specs=[rows_spec] * 3, out_shape=[rows_shape] * 3,
+    )(back, query_rows, out_grad, key_rows, value_rows, gain)
+    skip_grad = jnp.sum(skip_parts, axis=0) * factor
+    return (layer_out, query_grad, key_grad, value_grad, filter_grad, skip_grad)
 
 
 def rounded_trig(phase, modulus):
@@ -17,7 +279,7 @@
     return lax.all_to_all(blocks, ("outer", "inner"), split_axis=0, concat_axis=0, tiled=True)
 
 
-def body(query_rows, key_rows, value_rows, out_grad, filter_rows, skip_gain):
+def frequency_body(query_rows, key_rows, value_rows, out_grad, filter_rows, skip_gain):
     devices = lax.axis_size(("outer", "inner"))
     position = lax.axis_index(("outer", "inner"))
     tokens_here = query_rows.shape[0]
@@ -118,6 +380,11 @@
     return (layer_out, query_grad, key_grad, value_grad, filter_grad, skip_sum * factor)
 
 
+def body(*arrays):
+    lanes_full = arrays[0].shape[1] == lax.axis_size(AXES) * LANES
+    return (channel_body if lanes_full else frequency_body)(*arrays)
+
+
 def solution(mesh):
     return jax.shard_map(
         body,

time: 995 us -> 223 us (0.22)
  waiting for transfers between devices: 618 us -> 49.4 us
  local copies, waits for them, and re-layouts: 145 us -> 4.17 us
  Pallas kernels: 0 us -> 67.9 us
  other arithmetic: 62.9 us -> 0.96 us
  matrix products: 49.2 us -> 0 us
  blocking collectives: 91.6 us -> 80.7 us
    all_to_all x4, waiting for transfers between devices: 618 us -> 49.4 us  [exchange(): return lax.all_to_all(blocks, AXES, split_axis=0, concat_axis=0, tiled=True)]
    another operation x12 -> x0, local copies, waits for them, and re-layouts: 103 us -> none  [the longest x4 71.2 us: body(): section_one = regroup_blocks(jnp.stack(section_one, axis=2))]
    psum x1 -> x0, blocking collectives: 91.6 us -> none  [body(): skip_sum = lax.psum(skip_part, ('outer', 'inner'))]
    all_gather x0 -> x1, blocking collectives: none -> 80.7 us  [channel_body(): skip_parts = lax.all_gather(skip_part, AXES, axis=0, tiled=True)]
    pallas_call x0 -> x6, Pallas kernels: none -> 67.9 us  [the longest x1 25.4 us: channel_body(): pl.pallas_call(functools.partial(backward_kernel, tokens, scale, factor),...]
    another operation x16 -> x0, other arithmetic: 49.5 us -> none  [the longest x1 18 us: body(): jnp.stack(section_three, axis=2)]
    dot_general x7 -> x0, matrix products: 49.2 us -> none  [the longest x2 18 us: body(): jnp.einsum('oisbc,iosjk->jkbc', section_one[:, :, half], table_two, prefe...]
    squeeze x3 -> x0, local copies, waits for them, and re-layouts: 17.8 us -> none  [the longest x2 16.8 us: body(): spec_real, spec_imag = (spectra[0], spectra[1])]
  transfers between devices with their start and end apart: 4 -> 4, of which waited for: 3 -> 3; matrix products, arithmetic and copies ran while one was open for 0% -> 0% of each run, Pallas kernels for 0% -> 26%
where the time goes in v1:
time: 223 us; the launch traced here: 222 us
  blocking collectives  80.7 us (36%)
  Pallas kernels  67.9 us (30%)
  waiting for transfers between devices  49.4 us (22%)
  starting transfers between devices  18 us (8%)
  local copies, waits for them, and re-layouts  4.17 us (2%)
    all_gather x1, blocking collectives, channel_body(): skip_parts = lax.all_gather(skip_part, AXES, axis=0, tiled=True)  80.7 us
    all_to_all x4, waiting for transfers between devices, exchange(): return lax.all_to_all(blocks, AXES, split_axis=0, concat_axis=0, tiled=True)  49.4 us
    pallas_call x1, Pallas kernels, channel_body(): pl.pallas_call(functools.partial(backward_kernel, tokens, scale, factor),...  25.4 us
    pallas_call x1, Pallas kernels, channel_body(): pl.pallas_call(functools.partial(forward_kernel, tokens, scale), out_shap...  24.3 us
    all_to_all x4, starting transfers between devices, exchange(): return lax.all_to_all(blocks, AXES, split_axis=0, concat_axis=0, tiled=True)  18 us
    pallas_call x1, Pallas kernels, channel_body(): pl.pallas_call(carried_kernel, grid=grid, in_specs=[double_spec] + [rows_...  5.13 us
    pallas_call x1, Pallas kernels, channel_body(): pl.pallas_call(mixing_kernel, grid=grid, in_specs=[single_spec] + [rows_s...  4.74 us
  transfers between devices with their start and end apart: 4, of which 3 were waited for; matrix products, arithmetic and copies ran while one was open for 0% of the time, Pallas kernels for 26%

profile of v1, /device:TPU:0, one launch (start us, length us, event | category | flops | bytes accessed | tf_op | source)
XLA Modules:
  0.0 221.9 jit_solution(4654100561655974327)
XLA Ops:
  0.6 4.1 %shard_map.145 = bf16[32,256,128]{2,1,0:T(8,128)(2,1)} custom-call(bf16[128,4096]{1,0:T(8,128)(2,1)} %filter_ref.1, bf16[128,4096]{1,0:T(8,128)(2,1)} %key_ref.7, bf16[128,4096]{1,0:T(8,128)(2,1)} %value_ref.7), custom_call_target="tpu_custom_call" | custom-call | tf_op jit(solution)/shard_map/pallas_call | solution.py:229
  4.7 7.3 %all-to-all-start = ((bf16[32,256,128]{2,1,0:T(8,128)(2,1)}), bf16[32,256,128]{2,1,0:T(8,128)(2,1)S(1)}, u32[]{:S(2)}, u32[]{:S(2)}) async-start(bf16[32,256,128]{2,1,0:T(8,128)(2,1)} %shard_map.145), calls=%async_computation | async-start | bytes 4194304 | tf_op jit(solution)/shard_map/all_to_all | solution.py:204
  12.1 4.3 %shard_map.148 = (bf16[32,128,128]{2,1,0:T(8,128)(2,1)}, f32[1,4096]{1,0:T(1,128)}) custom-call(bf16[128,4096]{1,0:T(8,128)(2,1)} %query_ref.5, bf16[128,4096]{1,0:T(8,128)(2,1)} %grad_ref.5, bf16[128,4096]{1,0:T(8,128)(2,1)} %key_ref.7, bf16[128,4096]{1,0:T(8,128)(2,1)} %value_ref.7), custom_call_target="tpu_custom_call" | custom-call | tf_op jit(solution)/shard_map/pallas_call | solution.py:233
  16.3 0.0 copy-start
  16.3 45.8 %all-to-all-done.packed_ref = bf16[32,256,128]{2,1,0:T(8,128)(2,1)S(1)} async-done(((bf16[32,256,128]{2,1,0:T(8,128)(2,1)}), bf16[32,256,128]{2,1,0:T(8,128)(2,1)S(1)}, u32[]{:S(2)}, u32[]{:S(2)}) %all-to-all-start) | async-done | bytes 2097184 | tf_op jit(solution)/shard_map/all_to_all | solution.py:204
  62.2 2.6 %all-to-all-start.2 = ((bf16[32,128,128]{2,1,0:T(8,128)(2,1)}), bf16[32,128,128]{2,1,0:T(8,128)(2,1)S(1)}, u32[]{:S(2)}, u32[]{:S(2)}) async-start(bf16[32,128,128]{2,1,0:T(8,128)(2,1)} %get-tuple-element.18), calls=%async_computation.2 | async-start | bytes 2097152 | tf_op jit(solution)/shard_map/all_to_all | solution.py:204
  64.8 0.0 copy-done
  64.8 0.0 copy-start.2
  64.8 0.9 copy-done.2
  65.7 24.3 %shard_map.146 = (bf16[32,128,128]{2,1,0:T(8,128)(2,1)S(1)}, f32[33,256,256]{2,1,0:T(8,128)}) custom-call(bf16[32,256,128]{2,1,0:T(8,128)(2,1)S(1)} %all-to-all-done.packed_ref, bf16[16,528,256]{2,1,0:T(8,128)(2,1)} %constant.12.clone.first_ref, bf16[256,256]{1,0:T(8,128)(2,1)S(1)} %copy-done.2, bf16[33,256,256]{2,1,0:T(8,128)(2,1)} %constant.14.clone.third_ref, ...), custom_call_target="tpu_custom_call" | custom-call | tf_op jit(solution)/shard_map/pallas_call | solution.py:239
  90.0 0.0 copy-start.1
  90.0 1.0 copy-done.1
  91.0 0.0 copy-start.3
  91.0 1.4 all-to-all-done.2.gate_ref
  92.4 4.4 %all-to-all-start.1 = ((bf16[32,128,128]{2,1,0:T(8,128)(2,1)}), bf16[32,128,128]{2,1,0:T(8,128)(2,1)S(1)}, u32[]{:S(2)}, u32[]{:S(2)}) async-start(bf16[32,128,128]{2,1,0:T(8,128)(2,1)} %copy-done.1), calls=%async_computation.1 | async-start | bytes 2097152 | tf_op jit(solution)/shard_map/all_to_all | solution.py:204
  96.8 0.0 copy-done.3
  96.8 25.4 %shard_map.149 = bf16[32,256,128]{2,1,0:T(8,128)(2,1)} custom-call(bf16[32,128,128]{2,1,0:T(8,128)(2,1)S(1)} %all-to-all-done.2.gate_ref, f32[33,256,256]{2,1,0:T(8,128)} %get-tuple-element.19.spectra_ref, bf16[16,528,256]{2,1,0:T(8,128)(2,1)} %constant.12.clone.first_ref, bf16[256,256]{1,0:T(8,128)(2,1)S(1)} %copy-done.3, ...), custom_call_target="tpu_custom_call" | custom-call | tf_op jit(solution)/shard_map/pallas_call | solution.py:249
  122.2 0.0 copy-start.6
  122.2 2.2 all-to-all-done.1.conv_ref
  124.4 0.0 copy-start.5
  124.4 1.0 copy-done.5
  125.4 3.7 %all-to-all-start.3 = ((bf16[32,256,128]{2,1,0:T(8,128)(2,1)}), bf16[32,256,128]{2,1,0:T(8,128)(2,1)S(1)}, u32[]{:S(2)}, u32[]{:S(2)}) async-start(bf16[32,256,128]{2,1,0:T(8,128)(2,1)} %shard_map.149), calls=%async_computation.3 | async-start | bytes 4194304 | tf_op jit(solution)/shard_map/all_to_all | solution.py:204
  129.0 0.0 copy-done.6
  129.1 80.7 %all-gather = f32[32,1,4096]{2,1,0:T(1,128)S(1)} all-gather(f32[1,1,4096]{2,1,0:T(1,128)S(1)} %bitcast.4), channel_id=1, replica_groups=mesh['outer'=4,'inner'=8] {'outer','inner'}, dimensions={0}, use_global_device_ids=true | all-gather | bytes 540672 | tf_op jit(solution)/shard_map/all_gather | solution.py:237
  209.7 0.4 reduce_sum.9
  210.1 0.6 broadcast_multiply_fusion
  210.7 4.7 %shard_map.147 = (bf16[128,4096]{1,0:T(8,128)(2,1)}, bf16[128,4096]{1,0:T(8,128)(2,1)}) custom-call(bf16[32,128,128]{2,1,0:T(8,128)(2,1)} %copy-done.5, bf16[128,4096]{1,0:T(8,128)(2,1)} %query_ref.5, bf16[128,4096]{1,0:T(8,128)(2,1)} %grad_ref.5, bf16[128,4096]{1,0:T(8,128)(2,1)} %key_ref.7, bf16[128,4096]{1,0:T(8,128)(2,1)} %value_ref.7, f32[1,4096]{1,0:T(1,128)} %bitcast.2), custom_call_target="tpu_custom_call" | custom-call | tf_op jit(solution)/shard_map/pallas_call | solution.py:261
  215.4 0.0 all-to-all-done.3.back_ref
  215.4 0.0 copy-start.4
  215.4 1.3 copy-done.4
  216.8 5.1 %shard_map.150 = (bf16[128,4096]{1,0:T(8,128)(2,1)}, bf16[128,4096]{1,0:T(8,128)(2,1)}, bf16[128,4096]{1,0:T(8,128)(2,1)}) custom-call(bf16[32,256,128]{2,1,0:T(8,128)(2,1)} %copy-done.4, bf16[128,4096]{1,0:T(8,128)(2,1)} %query_ref.5, bf16[128,4096]{1,0:T(8,128)(2,1)} %grad_ref.5, bf16[128,4096]{1,0:T(8,128)(2,1)} %key_ref.7, bf16[128,4096]{1,0:T(8,128)(2,1)} %value_ref.7, ...), custom_call_target="tpu_custom_call" | custom-call | tf_op jit(solution)/shard_map/pallas_call | solution.py:265
Async XLA Ops:
  4.7 57.4 %all-to-all-start = ((bf16[32,256,128]{2,1,0:T(8,128)(2,1)}), bf16[32,256,128]{2,1,0:T(8,128)(2,1)S(1)}, u32[]{:S(2)}, u32[]{:S(2)}) async-start(bf16[32,256,128]{2,1,0:T(8,128)(2,1)} %shard_map.145), calls=%async_computation | async-start | bytes 4194304 | tf_op jit(solution)/shard_map/all_to_all | solution.py:204
  16.3 48.5 %copy-start = (bf16[256,528]{1,0:T(8,128)(2,1)S(1)}, bf16[256,528]{1,0:T(8,128)(2,1)}, u32[]{:S(2)}) copy-start(bf16[256,528]{1,0:T(8,128)(2,1)} %constant.15.clone.last_ref) | copy-start | bytes 811012
  62.2 30.2 %all-to-all-start.2 = ((bf16[32,128,128]{2,1,0:T(8,128)(2,1)}), bf16[32,128,128]{2,1,0:T(8,128)(2,1)S(1)}, u32[]{:S(2)}, u32[]{:S(2)}) async-start(bf16[32,128,128]{2,1,0:T(8,128)(2,1)} %get-tuple-element.18), calls=%async_computation.2 | async-start | bytes 2097152 | tf_op jit(solution)/shard_map/all_to_all | solution.py:204
  64.8 0.9 copy-start.2
  90.0 1.0 copy-start.1
  91.0 5.8 %copy-start.3 = (bf16[256,256]{1,0:T(8,128)(2,1)S(1)}, bf16[256,256]{1,0:T(8,128)(2,1)}, u32[]{:S(2)}) copy-start(bf16[256,256]{1,0:T(8,128)(2,1)} %constant.13.clone.second_ref) | copy-start | bytes 393220
  92.4 32.0 %all-to-all-start.1 = ((bf16[32,128,128]{2,1,0:T(8,128)(2,1)}), bf16[32,128,128]{2,1,0:T(8,128)(2,1)S(1)}, u32[]{:S(2)}, u32[]{:S(2)}) async-start(bf16[32,128,128]{2,1,0:T(8,128)(2,1)} %copy-done.1), calls=%async_computation.1 | async-start | bytes 2097152 | tf_op jit(solution)/shard_map/all_to_all | solution.py:204
  122.2 6.8 %copy-start.6 = (f32[1,4096]{1,0:T(1,128)S(1)}, f32[1,4096]{1,0:T(1,128)}, u32[]{:S(2)}) copy-start(f32[1,4096]{1,0:T(1,128)} %get-tuple-element.23) | copy-start | bytes 49156
  124.4 1.0 copy-start.5
  125.4 90.1 %all-to-all-start.3 = ((bf16[32,256,128]{2,1,0:T(8,128)(2,1)}), bf16[32,256,128]{2,1,0:T(8,128)(2,1)S(1)}, u32[]{:S(2)}, u32[]{:S(2)}) async-start(bf16[32,256,128]{2,1,0:T(8,128)(2,1)} %shard_map.149), calls=%async_computation.3 | async-start | bytes 4194304 | tf_op jit(solution)/shard_map/all_to_all | solution.py:204
  215.4 1.3 copy-start.4

commit v2 on v1

--- a/solution.py
+++ b/solution.py
@@ -204,6 +204,15 @@
     return lax.all_to_all(blocks, AXES, split_axis=0, concat_axis=0, tiled=True)
 
 
+def total_of(part):
+    devices = lax.axis_size(AXES)
+    step = 1
+    while step < devices:
+        part = part + lax.ppermute(part, AXES, [(d, d ^ step) for d in range(devices)])
+        step *= 2
+    return part
+
+
 def limit(mib):
     return pltpu.CompilerParams(vmem_limit_bytes=mib * 1024 * 1024)
 
@@ -234,7 +243,7 @@
         gate_kernel, grid=grid, in_specs=[rows_spec] * 4, out_specs=[single_spec, vector_spec],
         out_shape=[single_shape, jax.ShapeDtypeStruct((1, channels), F32)],
     )(query_rows, out_grad, key_rows, value_rows)
-    skip_parts = lax.all_gather(skip_part, AXES, axis=0, tiled=True)
+    skip_total = total_of(skip_part)
     gate = exchange(gate)
     convolved, spectra = pl.pallas_call(
         functools.partial(forward_kernel, tokens, scale),
@@ -266,7 +275,7 @@
         carried_kernel, grid=grid, in_specs=[double_spec] + [rows_spec] * 4 + [vector_spec],
         out_specs=[rows_spec] * 3, out_shape=[rows_shape] * 3,
     )(back, query_rows, out_grad, key_rows, value_rows, gain)
-    skip_grad = jnp.sum(skip_parts, axis=0) * factor
+    skip_grad = skip_total[0] * factor
     return (layer_out, query_grad, key_grad, value_grad, filter_grad, skip_grad)
 
 

time: 223 us -> 199 us (0.89)
  blocking collectives: 80.7 us -> 0 us
  waiting for transfers between devices: 49.4 us -> 96.7 us
  starting transfers between devices: 18 us -> 27.8 us
    all_gather x1 -> x0, blocking collectives: 80.7 us -> none  [channel_body(): skip_parts = lax.all_gather(skip_part, AXES, axis=0, tiled=True)]
    ppermute x0 -> x5, waiting for transfers between devices: none -> 47.3 us  [total_of(): lax.ppermute(part, AXES, [(d, d ^ step) for d in range(devices)])]
    ppermute x0 -> x5, starting transfers between devices: none -> 9.76 us  [total_of(): lax.ppermute(part, AXES, [(d, d ^ step) for d in range(devices)])]
  transfers between devices with their start and end apart: 4 -> 9, of which waited for: 3 -> 8; matrix products, arithmetic and copies ran while one was open for 0% -> 0% of each run, Pallas kernels for 26% -> 30%
where the time goes in v2:
time: 199 us; the launch traced here: 198 us
  waiting for transfers between devices  96.7 us (49%)
  Pallas kernels  68 us (34%)
  starting transfers between devices  27.8 us (14%)
  local copies, waits for them, and re-layouts  4.17 us (2%)
    all_to_all x4, waiting for transfers between devices, exchange(): return lax.all_to_all(blocks, AXES, split_axis=0, concat_axis=0, tiled=True)  49.4 us
    ppermute x5, waiting for transfers between devices, total_of(): lax.ppermute(part, AXES, [(d, d ^ step) for d in range(devices)])  47.3 us
    pallas_call x1, Pallas kernels, channel_body(): pl.pallas_call(functools.partial(backward_kernel, tokens, scale, factor),...  25.4 us
    pallas_call x1, Pallas kernels, channel_body(): pl.pallas_call(functools.partial(forward_kernel, tokens, scale), out_shap...  24.3 us
    all_to_all x4, starting transfers between devices, exchange(): return lax.all_to_all(blocks, AXES, split_axis=0, concat_axis=0, tiled=True)  18.1 us
    ppermute x5, starting transfers between devices, total_of(): lax.ppermute(part, AXES, [(d, d ^ step) for d in range(devices)])  9.76 us
    pallas_call x1, Pallas kernels, channel_body(): pl.pallas_call(carried_kernel, grid=grid, in_specs=[double_spec] + [rows_...  5.13 us
    pallas_call x1, Pallas kernels, channel_body(): pl.pallas_call(mixing_kernel, grid=grid, in_specs=[single_spec] + [rows_s...  4.74 us
  transfers between devices with their start and end apart: 9, of which 8 were waited for; matrix products, arithmetic and copies ran while one was open for 0% of the time, Pallas kernels for 30%

profile of v2, /device:TPU:0, one launch (start us, length us, event | category | flops | bytes accessed | tf_op | source)
XLA Modules:
  0.0 198.1 jit_solution(5705796566793988536)
XLA Ops:
  0.6 4.1 %shard_map.145 = bf16[32,256,128]{2,1,0:T(8,128)(2,1)} custom-call(bf16[128,4096]{1,0:T(8,128)(2,1)} %filter_ref.1, bf16[128,4096]{1,0:T(8,128)(2,1)} %key_ref.7, bf16[128,4096]{1,0:T(8,128)(2,1)} %value_ref.7), custom_call_target="tpu_custom_call" | custom-call | tf_op jit(solution)/shard_map/pallas_call | solution.py:238
  4.7 7.3 %all-to-all-start = ((bf16[32,256,128]{2,1,0:T(8,128)(2,1)}), bf16[32,256,128]{2,1,0:T(8,128)(2,1)S(1)}, u32[]{:S(2)}, u32[]{:S(2)}) async-start(bf16[32,256,128]{2,1,0:T(8,128)(2,1)} %shard_map.145), calls=%async_computation | async-start | bytes 4194304 | tf_op jit(solution)/shard_map/all_to_all | solution.py:204
  12.0 4.3 %shard_map.148 = (bf16[32,128,128]{2,1,0:T(8,128)(2,1)}, f32[1,4096]{1,0:T(1,128)}) custom-call(bf16[128,4096]{1,0:T(8,128)(2,1)} %query_ref.5, bf16[128,4096]{1,0:T(8,128)(2,1)} %grad_ref.5, bf16[128,4096]{1,0:T(8,128)(2,1)} %key_ref.7, bf16[128,4096]{1,0:T(8,128)(2,1)} %value_ref.7), custom_call_target="tpu_custom_call" | custom-call | tf_op jit(solution)/shard_map/pallas_call | solution.py:242
  16.3 0.0 copy-start
  16.3 45.8 %all-to-all-done.packed_ref = bf16[32,256,128]{2,1,0:T(8,128)(2,1)S(1)} async-done(((bf16[32,256,128]{2,1,0:T(8,128)(2,1)}), bf16[32,256,128]{2,1,0:T(8,128)(2,1)S(1)}, u32[]{:S(2)}, u32[]{:S(2)}) %all-to-all-start) | async-done | bytes 2097184 | tf_op jit(solution)/shard_map/all_to_all | solution.py:204
  62.1 2.6 %all-to-all-start.2 = ((bf16[32,128,128]{2,1,0:T(8,128)(2,1)}), bf16[32,128,128]{2,1,0:T(8,128)(2,1)S(1)}, u32[]{:S(2)}, u32[]{:S(2)}) async-start(bf16[32,128,128]{2,1,0:T(8,128)(2,1)} %get-tuple-element.18), calls=%async_computation.2 | async-start | bytes 2097152 | tf_op jit(solution)/shard_map/all_to_all | solution.py:204
  64.8 0.0 copy-done
  64.8 0.0 copy-start.2
  64.8 0.9 copy-done.2
  65.7 24.3 %shard_map.146 = (bf16[32,128,128]{2,1,0:T(8,128)(2,1)S(1)}, f32[33,256,256]{2,1,0:T(8,128)}) custom-call(bf16[32,256,128]{2,1,0:T(8,128)(2,1)S(1)} %all-to-all-done.packed_ref, bf16[16,528,256]{2,1,0:T(8,128)(2,1)} %constant.10.clone.first_ref, bf16[256,256]{1,0:T(8,128)(2,1)S(1)} %copy-done.2, bf16[33,256,256]{2,1,0:T(8,128)(2,1)} %constant.12.clone.third_ref, ...), custom_call_target="tpu_custom_call" | custom-call | tf_op jit(solution)/shard_map/pallas_call | solution.py:248
  90.0 0.0 copy-start.1
  90.0 1.0 copy-done.1
  91.0 0.0 copy-start.3
  91.0 1.4 all-to-all-done.2.gate_ref
  92.4 4.4 %all-to-all-start.1 = ((bf16[32,128,128]{2,1,0:T(8,128)(2,1)}), bf16[32,128,128]{2,1,0:T(8,128)(2,1)S(1)}, u32[]{:S(2)}, u32[]{:S(2)}) async-start(bf16[32,128,128]{2,1,0:T(8,128)(2,1)} %copy-done.1), calls=%async_computation.1 | async-start | bytes 2097152 | tf_op jit(solution)/shard_map/all_to_all | solution.py:204
  96.8 0.0 copy-done.3
  96.8 25.4 %shard_map.149 = bf16[32,256,128]{2,1,0:T(8,128)(2,1)} custom-call(bf16[32,128,128]{2,1,0:T(8,128)(2,1)S(1)} %all-to-all-done.2.gate_ref, f32[33,256,256]{2,1,0:T(8,128)} %get-tuple-element.19.spectra_ref, bf16[16,528,256]{2,1,0:T(8,128)(2,1)} %constant.10.clone.first_ref, bf16[256,256]{1,0:T(8,128)(2,1)S(1)} %copy-done.3, ...), custom_call_target="tpu_custom_call" | custom-call | tf_op jit(solution)/shard_map/pallas_call | solution.py:258
  122.3 0.0 copy-start.6
  122.3 2.2 %all-to-all-done.1.conv_ref = bf16[32,128,128]{2,1,0:T(8,128)(2,1)S(1)} async-done(((bf16[32,128,128]{2,1,0:T(8,128)(2,1)}), bf16[32,128,128]{2,1,0:T(8,128)(2,1)S(1)}, u32[]{:S(2)}, u32[]{:S(2)}) %all-to-all-start.1) | async-done | bytes 1048608 | tf_op jit(solution)/shard_map/all_to_all | solution.py:204
  124.4 0.0 copy-start.5
  124.4 1.0 copy-done.5
  125.4 3.7 %all-to-all-start.3 = ((bf16[32,256,128]{2,1,0:T(8,128)(2,1)}), bf16[32,256,128]{2,1,0:T(8,128)(2,1)S(1)}, u32[]{:S(2)}, u32[]{:S(2)}) async-start(bf16[32,256,128]{2,1,0:T(8,128)(2,1)} %shard_map.149), calls=%async_computation.3 | async-start | bytes 4194304 | tf_op jit(solution)/shard_map/all_to_all | solution.py:204
  129.1 0.0 copy-done.6
  129.1 0.3 collective-permute-start
  129.4 0.9 collective-permute-done
  130.4 1.8 collective-permute-start.1
  132.2 31.8 %collective-permute-done.1 = f32[1,4096]{1,0:T(1,128)S(1)} collective-permute-done((f32[1,4096]{1,0:T(1,128)S(1)}, f32[1,4096]{1,0:T(1,128)S(1)}, u32[]{:S(2)}, u32[]{:S(2)}) %collective-permute-start.1) | collective-permute-done | bytes 16416 | tf_op jit(solution)/shard_map/ppermute | solution.py:211
  164.0 4.6 %collective-permute-start.2 = (f32[1,4096]{1,0:T(1,128)S(1)}, f32[1,4096]{1,0:T(1,128)S(1)}, u32[]{:S(2)}, u32[]{:S(2)}) collective-permute-start(f32[1,4096]{1,0:T(1,128)S(1)} %add.16), channel_id=1, source_target_pairs={{0,4},{1,5},{2,6},{3,7},{4,0},{5,1},{6,2},{7,3},{8,12},{9,13},{10,... | collective-permute-start | bytes 49160 | tf_op jit(solution)/shard_map/ppermute | solution.py:211
  168.7 9.9 %collective-permute-done.2 = f32[1,4096]{1,0:T(1,128)S(1)} collective-permute-done((f32[1,4096]{1,0:T(1,128)S(1)}, f32[1,4096]{1,0:T(1,128)S(1)}, u32[]{:S(2)}, u32[]{:S(2)}) %collective-permute-start.2) | collective-permute-done | bytes 16416 | tf_op jit(solution)/shard_map/ppermute | solution.py:211
  178.6 1.5 collective-permute-start.3
  180.1 2.3 %collective-permute-done.3 = f32[1,4096]{1,0:T(1,128)S(1)} collective-permute-done((f32[1,4096]{1,0:T(1,128)S(1)}, f32[1,4096]{1,0:T(1,128)S(1)}, u32[]{:S(2)}, u32[]{:S(2)}) %collective-permute-start.3) | collective-permute-done | bytes 16416 | tf_op jit(solution)/shard_map/ppermute | solution.py:211
  182.4 1.5 collective-permute-start.4
  183.9 2.3 %collective-permute-done.4 = f32[1,4096]{1,0:T(1,128)S(1)} collective-permute-done((f32[1,4096]{1,0:T(1,128)S(1)}, f32[1,4096]{1,0:T(1,128)S(1)}, u32[]{:S(2)}, u32[]{:S(2)}) %collective-permute-start.4) | collective-permute-done | bytes 16416 | tf_op jit(solution)/shard_map/ppermute | solution.py:211
  186.2 0.6 add_multiply_fusion
  186.9 4.7 %shard_map.147 = (bf16[128,4096]{1,0:T(8,128)(2,1)}, bf16[128,4096]{1,0:T(8,128)(2,1)}) custom-call(bf16[32,128,128]{2,1,0:T(8,128)(2,1)} %copy-done.5, bf16[128,4096]{1,0:T(8,128)(2,1)} %query_ref.5, bf16[128,4096]{1,0:T(8,128)(2,1)} %grad_ref.5, bf16[128,4096]{1,0:T(8,128)(2,1)} %key_ref.7, bf16[128,4096]{1,0:T(8,128)(2,1)} %value_ref.7, f32[1,4096]{1,0:T(1,128)} %bitcast.2), custom_call_target="tpu_custom_call" | custom-call | tf_op jit(solution)/shard_map/pallas_call | solution.py:270
  191.6 0.0 all-to-all-done.3.back_ref
  191.6 0.0 copy-start.4
  191.6 1.3 copy-done.4
  192.9 5.1 %shard_map.150 = (bf16[128,4096]{1,0:T(8,128)(2,1)}, bf16[128,4096]{1,0:T(8,128)(2,1)}, bf16[128,4096]{1,0:T(8,128)(2,1)}) custom-call(bf16[32,256,128]{2,1,0:T(8,128)(2,1)} %copy-done.4, bf16[128,4096]{1,0:T(8,128)(2,1)} %query_ref.5, bf16[128,4096]{1,0:T(8,128)(2,1)} %grad_ref.5, bf16[128,4096]{1,0:T(8,128)(2,1)} %key_ref.7, bf16[128,4096]{1,0:T(8,128)(2,1)} %value_ref.7, ...), custom_call_target="tpu_custom_call" | custom-call | tf_op jit(solution)/shard_map/pallas_call | solution.py:274
  (4 shorter events, 0.1 us)
Async XLA Ops:
  4.7 57.4 %all-to-all-start = ((bf16[32,256,128]{2,1,0:T(8,128)(2,1)}), bf16[32,256,128]{2,1,0:T(8,128)(2,1)S(1)}, u32[]{:S(2)}, u32[]{:S(2)}) async-start(bf16[32,256,128]{2,1,0:T(8,128)(2,1)} %shard_map.145), calls=%async_computation | async-start | bytes 4194304 | tf_op jit(solution)/shard_map/all_to_all | solution.py:204
  16.3 48.5 %copy-start = (bf16[256,528]{1,0:T(8,128)(2,1)S(1)}, bf16[256,528]{1,0:T(8,128)(2,1)}, u32[]{:S(2)}) copy-start(bf16[256,528]{1,0:T(8,128)(2,1)} %constant.13.clone.last_ref) | copy-start | bytes 811012
  62.1 30.2 %all-to-all-start.2 = ((bf16[32,128,128]{2,1,0:T(8,128)(2,1)}), bf16[32,128,128]{2,1,0:T(8,128)(2,1)S(1)}, u32[]{:S(2)}, u32[]{:S(2)}) async-start(bf16[32,128,128]{2,1,0:T(8,128)(2,1)} %get-tuple-element.18), calls=%async_computation.2 | async-start | bytes 2097152 | tf_op jit(solution)/shard_map/all_to_all | solution.py:204
  64.8 0.9 copy-start.2
  90.0 1.0 copy-start.1
  91.0 5.8 %copy-start.3 = (bf16[256,256]{1,0:T(8,128)(2,1)S(1)}, bf16[256,256]{1,0:T(8,128)(2,1)}, u32[]{:S(2)}) copy-start(bf16[256,256]{1,0:T(8,128)(2,1)} %constant.11.clone.second_ref) | copy-start | bytes 393220
  92.4 32.0 %all-to-all-start.1 = ((bf16[32,128,128]{2,1,0:T(8,128)(2,1)}), bf16[32,128,128]{2,1,0:T(8,128)(2,1)S(1)}, u32[]{:S(2)}, u32[]{:S(2)}) async-start(bf16[32,128,128]{2,1,0:T(8,128)(2,1)} %copy-done.1), calls=%async_computation.1 | async-start | bytes 2097152 | tf_op jit(solution)/shard_map/all_to_all | solution.py:204
  122.3 6.8 %copy-start.6 = (f32[1,4096]{1,0:T(1,128)S(1)}, f32[1,4096]{1,0:T(1,128)}, u32[]{:S(2)}) copy-start(f32[1,4096]{1,0:T(1,128)} %get-tuple-element.23) | copy-start | bytes 49156
  124.4 1.0 copy-start.5
  125.4 66.2 %all-to-all-start.3 = ((bf16[32,256,128]{2,1,0:T(8,128)(2,1)}), bf16[32,256,128]{2,1,0:T(8,128)(2,1)S(1)}, u32[]{:S(2)}, u32[]{:S(2)}) async-start(bf16[32,256,128]{2,1,0:T(8,128)(2,1)} %shard_map.149), calls=%async_computation.3 | async-start | bytes 4194304 | tf_op jit(solution)/shard_map/all_to_all | solution.py:204
  129.1 1.2 collective-permute-start
  130.4 33.7 %collective-permute-start.1 = (f32[1,4096]{1,0:T(1,128)S(1)}, f32[1,4096]{1,0:T(1,128)S(1)}, u32[]{:S(2)}, u32[]{:S(2)}) collective-permute-start(f32[1,4096]{1,0:T(1,128)S(1)} %add.15), channel_id=1, source_target_pairs={{0,2},{1,3},{2,0},{3,1},{4,6},{5,7},{6,4},{7,5},{8,10},{9,11},{10,... | collective-permute-start | bytes 49160 | tf_op jit(solution)/shard_map/ppermute | solution.py:211
  164.0 14.6 %collective-permute-start.2 = (f32[1,4096]{1,0:T(1,128)S(1)}, f32[1,4096]{1,0:T(1,128)S(1)}, u32[]{:S(2)}, u32[]{:S(2)}) collective-permute-start(f32[1,4096]{1,0:T(1,128)S(1)} %add.16), channel_id=1, source_target_pairs={{0,4},{1,5},{2,6},{3,7},{4,0},{5,1},{6,2},{7,3},{8,12},{9,13},{10,... | collective-permute-start | bytes 49160 | tf_op jit(solution)/shard_map/ppermute | solution.py:211
  178.6 3.8 %collective-permute-start.3 = (f32[1,4096]{1,0:T(1,128)S(1)}, f32[1,4096]{1,0:T(1,128)S(1)}, u32[]{:S(2)}, u32[]{:S(2)}) collective-permute-start(f32[1,4096]{1,0:T(1,128)S(1)} %add.17), channel_id=1, source_target_pairs={{0,8},{1,9},{2,10},{3,11},{4,12},{5,13},{6,14},{7,15},{8,0},{9,1},... | collective-permute-start | bytes 49160 | tf_op jit(solution)/shard_map/ppermute | solution.py:211
  182.4 3.8 %collective-permute-start.4 = (f32[1,4096]{1,0:T(1,128)S(1)}, f32[1,4096]{1,0:T(1,128)S(1)}, u32[]{:S(2)}, u32[]{:S(2)}) collective-permute-start(f32[1,4096]{1,0:T(1,128)S(1)} %add.18), channel_id=1, source_target_pairs={{0,16},{1,17},{2,18},{3,19},{4,20},{5,21},{6,22},{7,23},{8,24},{9,... | collective-permute-start | bytes 49160 | tf_op jit(solution)/shard_map/ppermute | solution.py:211
  191.6 1.3 copy-start.4

commit v3 on v0

--- a/solution.py
+++ b/solution.py
@@ -1,11 +1,304 @@
+import functools
 import math
 
 import jax
 import jax.numpy as jnp
+import ml_dtypes
+import numpy as np
 from jax import lax
+from jax.experimental import pallas as pl
+from jax.experimental.pallas import tpu as pltpu
 from jax.sharding import PartitionSpec as P
 
 TWO_PI = 2.0 * math.pi
+AXES = ("outer", "inner")
+LANES = 128
+SUBLANES = 8
+SPARE = 2 * SUBLANES
+BF16 = jnp.bfloat16
+F32 = jnp.float32
+
+
+def table_trig(phase, modulus):
+    angle = (phase % modulus).astype(np.float32) * np.float32(TWO_PI / modulus)
+    return tuple(
+        part.astype(ml_dtypes.bfloat16).astype(np.float32) for part in (np.cos(angle), np.sin(angle))
+    )
+
+
+def make_tables(rows, steps):
+    planes = rows + 1
+    points = 2 * rows * steps
+    row = np.arange(rows)
+    plane = np.arange(planes)
+    step = np.arange(steps)
+    eye = np.eye(SUBLANES, dtype=np.float32)
+    phase = row[None, None, :] * plane[None, :, None] * steps + step[:, None, None] * plane[None, :, None]
+    cos, sin = table_trig(phase, points)
+    first = np.stack([cos, -sin], axis=1).reshape(steps // SUBLANES, SUBLANES, 2, planes, rows)
+    first = np.einsum("bipkr,ij->bpkirj", first, eye)
+    first = first.reshape(steps // SUBLANES, 2 * planes * SUBLANES, rows * SUBLANES)
+    cos, sin = table_trig(step[:, None] * step[None, :], steps)
+    second = np.block([[cos, sin], [-sin, cos]])
+    phase = step[None, :, None] * step[None, None, :] * (2 * rows) + step[None, :, None] * plane[:, None, None]
+    cos, sin = table_trig(phase, points)
+    third = np.concatenate(
+        [np.concatenate([cos, -sin], axis=2), np.concatenate([sin, cos], axis=2)], axis=1
+    )
+    cos, sin = table_trig(row[:, None] * plane[None, :], 2 * rows)
+    weight = np.where((plane == 0) | (plane == rows), 1.0, 2.0).astype(np.float32)
+    last = np.stack([cos * weight, -sin * weight], axis=1)
+    last = np.einsum("rpk,ij->ripkj", last, eye).reshape(rows * SUBLANES, 2 * planes * SUBLANES)
+    return tuple(table.astype(ml_dtypes.bfloat16) for table in (first, second, third, last))
+
+
+def dot(a, b):
+    return jnp.dot(a, b, preferred_element_type=F32)
+
+
+def product_of(key, value):
+    return (key.astype(F32) * value.astype(F32)).astype(BF16)
+
+
+def row_group(b, size=2 * SUBLANES):
+    return pl.ds(pl.multiple_of(b * size, size), size)
+
+
+def pack_kernel(filter_ref, key_ref, value_ref, out_ref):
+    tokens = filter_ref.shape[0]
+    for d in range(out_ref.shape[0]):
+        cols = pl.ds(d * LANES, LANES)
+        out_ref[d, :tokens, :] = filter_ref[:, cols]
+        out_ref[d, tokens:, :] = product_of(key_ref[:, cols], value_ref[:, cols])
+
+
+def gate_kernel(query_ref, grad_ref, out_ref):
+    for d in range(out_ref.shape[0]):
+        cols = pl.ds(d * LANES, LANES)
+        out_ref[d] = (grad_ref[:, cols].astype(F32) * query_ref[:, cols].astype(F32)).astype(BF16)
+
+
+def looped(count, chunk, one):
+    def several(i, _):
+        for j in range(chunk):
+            one(i * chunk + j)
+        return 0
+
+    lax.fori_loop(0, count // chunk, several, 0)
+    for i in range(count - count % chunk, count):
+        one(i)
+
+
+def spectrum_of(read, first_ref, second_ref, section, store):
+    planes, steps, width = section.shape[0], section.shape[1] // 2, section.shape[2]
+
+    def one(b):
+        pair = read(b)
+        for half in range(2):
+            block = pair[:, half * SUBLANES : (half + 1) * SUBLANES, :]
+            result = dot(first_ref[2 * b + half], block.reshape(-1, width).astype(BF16))
+            result = result.reshape(2, planes, SUBLANES, width)
+            section[:, row_group(2 * b + half, SUBLANES), :] = result[0]
+            section[:, row_group(2 * b + half + steps // SUBLANES, SUBLANES), :] = result[1]
+
+    looped(steps // (2 * SUBLANES), 2, one)
+
+    def two(k):
+        store(k, dot(second_ref[...], section[k].astype(BF16)))
+
+    looped(planes, 8, two)
+
+
+def inverse_of(product_at, third_ref, last_ref, section, scale, write):
+    planes, steps, width = section.shape[0], section.shape[1] // 2, section.shape[2]
+
+    def three(k):
+        section[k] = dot(third_ref[k], product_at(k))
+
+    looped(planes, 8, three)
+
+    def four(b):
+        halves = []
+        for half in range(2):
+            real = section[:, row_group(2 * b + half, SUBLANES), :].reshape(-1, width)
+            imag = section[:, row_group(2 * b + half + steps // SUBLANES, SUBLANES), :].reshape(-1, width)
+            flat = jnp.concatenate([real, imag], axis=0).astype(BF16)
+            halves.append((dot(last_ref[...], flat) * scale).reshape(-1, SUBLANES, width))
+        write(b, jnp.concatenate(halves, axis=1).astype(BF16))
+
+    looped(steps // (2 * SUBLANES), 2, four)
+
+
+def parts_of(plane):
+    steps = plane.shape[0] // 2
+    return plane[:steps], plane[steps:]
+
+
+def conj_product(a, b):
+    (ar, ai), (br, bi) = parts_of(a), parts_of(b)
+    return jnp.concatenate([ar * br + ai * bi, ar * bi - ai * br], axis=0)
+
+
+def forward_kernel(scale, packed_ref, first_ref, second_ref, third_ref, last_ref, out_ref, spectra_ref, wide, narrow):
+    pairs = packed_ref.shape[1] // (4 * SUBLANES)
+
+    def read(b):
+        filt, value = packed_ref[:, row_group(b), :], packed_ref[:, row_group(b + pairs), :]
+        return jnp.concatenate([filt.astype(F32), value.astype(F32)], axis=2)
+
+    def store(k, plane):
+        spectra_ref[k] = plane
+
+    spectrum_of(read, first_ref, second_ref, wide, store)
+
+    def product_at(k):
+        (fr, fi), (vr, vi) = parts_of(spectra_ref[k, :, :LANES]), parts_of(spectra_ref[k, :, LANES:])
+        return jnp.concatenate([vr * fr - vi * fi, vr * fi + vi * fr], axis=0).astype(BF16)
+
+    def write(b, rows):
+        out_ref[:, row_group(b), :] = rows
+
+    inverse_of(product_at, third_ref, last_ref, narrow, scale, write)
+
+
+def split_rows(total):
+    rows = []
+    for _ in range(3):
+        rows.append(total.astype(BF16).astype(F32))
+        total = total - rows[-1]
+    rows.append(jnp.zeros((SPARE - len(rows), total.shape[1]), F32))
+    return jnp.concatenate(rows, axis=0).astype(BF16)
+
+
+def backward_kernel(scale, factor, gate_ref, packed_ref, spectra_ref, first_ref, second_ref, third_ref, last_ref, out_ref, section, gate_spectrum, wide):
+    steps = gate_ref.shape[1]
+    pairs = steps // (2 * SUBLANES)
+
+    def gate_times_product(d, total):
+        return total + gate_ref[d].astype(F32) * packed_ref[d, steps:, :].astype(F32)
+
+    total = lax.fori_loop(0, gate_ref.shape[0], gate_times_product, jnp.zeros((steps, LANES), F32))
+    spare = split_rows(jnp.sum(total, axis=0, keepdims=True) * factor)
+    for d in range(out_ref.shape[0]):
+        out_ref[d, 2 * steps :, :] = spare
+
+    def read(b):
+        return gate_ref[:, row_group(b), :].astype(F32)
+
+    def store(k, plane):
+        gate_spectrum[k] = plane
+
+    spectrum_of(read, first_ref, second_ref, section, store)
+
+    def product_at(k):
+        gate = gate_spectrum[k]
+        back = conj_product(spectra_ref[k, :, :LANES], gate)
+        lag = conj_product(spectra_ref[k, :, LANES:], gate) * factor
+        return jnp.concatenate([back, lag], axis=1).astype(BF16)
+
+    def write(b, rows):
+        out_ref[:, row_group(b), :] = rows[:, :, :LANES]
+        out_ref[:, row_group(b + pairs), :] = rows[:, :, LANES:]
+
+    inverse_of(product_at, third_ref, last_ref, wide, scale, write)
+
+
+def mixing_kernel(conv_ref, query_ref, grad_ref, key_ref, value_ref, gain_ref, layer_ref, query_grad_ref):
+    for d in range(conv_ref.shape[0]):
+        cols = pl.ds(d * LANES, LANES)
+        product = product_of(key_ref[:, cols], value_ref[:, cols]).astype(F32)
+        mixing = conv_ref[d].astype(F32) + gain_ref[:, cols] * product
+        layer_ref[:, cols] = (query_ref[:, cols].astype(F32) * mixing).astype(BF16)
+        query_grad_ref[:, cols] = (grad_ref[:, cols].astype(F32) * mixing).astype(BF16)
+
+
+def carried_kernel(back_ref, query_ref, grad_ref, key_ref, value_ref, gain_ref, key_grad_ref, value_grad_ref, filter_grad_ref, skip_ref):
+    tokens = query_ref.shape[0]
+    for d in range(back_ref.shape[0]):
+        cols = pl.ds(d * LANES, LANES)
+        gate = grad_ref[:, cols].astype(F32) * query_ref[:, cols].astype(F32)
+        carried = back_ref[d, :tokens, :].astype(F32) + gain_ref[:, cols] * gate
+        key_grad_ref[:, cols] = (carried * value_ref[:, cols].astype(F32)).astype(BF16)
+        value_grad_ref[:, cols] = (carried * key_ref[:, cols].astype(F32)).astype(BF16)
+        filter_grad_ref[:, cols] = back_ref[d, tokens : 2 * tokens, :]
+        spare = back_ref[d, 2 * tokens :, :].astype(F32)
+        skip_ref[:, cols] = jnp.sum(spare, axis=0, keepdims=True)
+
+
+def exchange(blocks):
+    return lax.all_to_all(blocks, AXES, split_axis=0, concat_axis=0, tiled=True)
+
+
+def limit(mib):
+    return pltpu.CompilerParams(vmem_limit_bytes=mib * 1024 * 1024)
+
+
+def kernel(body, *arrays, after=(), in_specs=None, **options):
+    count, waits = len(arrays), len(after)
+
+    def waiting(*refs):
+        body(*refs[:count], *refs[count + waits :])
+
+    specs = list(in_specs or [pl.BlockSpec()] * count) + [pl.BlockSpec(memory_space=pl.ANY)] * waits
+    return pl.pallas_call(waiting, in_specs=specs, **options)(*arrays, *after)
+
+
+def channel_body(query_rows, key_rows, value_rows, out_grad, filter_rows, skip_gain):
+    devices = lax.axis_size(AXES)
+    tokens, channels = query_rows.shape
+    length = tokens * devices
+    factor = 1.0 / math.sqrt(length)
+    scale = 1.0 / (2 * length)
+    planes = devices + 1
+    tables = [jnp.asarray(table) for table in make_tables(devices, tokens)]
+    blocks = math.gcd(devices, 8)
+    grid = (devices // blocks,)
+    back_rows = 2 * tokens + SPARE
+    rows_spec = pl.BlockSpec((tokens, blocks * LANES), lambda i: (0, i))
+    vector_spec = pl.BlockSpec((1, blocks * LANES), lambda i: (0, i))
+    single_spec = pl.BlockSpec((blocks, tokens, LANES), lambda i: (i, 0, 0))
+    double_spec = pl.BlockSpec((blocks, 2 * tokens, LANES), lambda i: (i, 0, 0))
+    back_spec = pl.BlockSpec((blocks, back_rows, LANES), lambda i: (i, 0, 0))
+    rows_shape = jax.ShapeDtypeStruct((tokens, channels), BF16)
+    single_shape = jax.ShapeDtypeStruct((devices, tokens, LANES), BF16)
+    double_shape = jax.ShapeDtypeStruct((devices, 2 * tokens, LANES), BF16)
+    back_shape = jax.ShapeDtypeStruct((devices, back_rows, LANES), BF16)
+    narrow = pltpu.VMEM((planes, 2 * tokens, LANES), F32)
+    wide = pltpu.VMEM((planes, 2 * tokens, 2 * LANES), F32)
+
+    packed = kernel(
+        pack_kernel, filter_rows, key_rows, value_rows, grid=grid,
+        in_specs=[rows_spec] * 3, out_specs=double_spec, out_shape=double_shape,
+    )
+    gate = kernel(
+        gate_kernel, query_rows, out_grad, after=[packed], grid=grid,
+        in_specs=[rows_spec] * 2, out_specs=single_spec, out_shape=single_shape,
+    )
+    packed = exchange(packed)
+    gate = exchange(gate)
+    convolved, spectra = kernel(
+        functools.partial(forward_kernel, scale), packed, *tables,
+        out_shape=[single_shape, jax.ShapeDtypeStruct((planes, 2 * tokens, 2 * LANES), F32)],
+        scratch_shapes=[wide, narrow], compiler_params=limit(48),
+    )
+    convolved = exchange(convolved)
+    back = kernel(
+        functools.partial(backward_kernel, scale, factor), gate, packed, spectra, *tables,
+        out_shape=back_shape, scratch_shapes=[narrow, narrow, wide], compiler_params=limit(52),
+    )
+    back = exchange(back)
+    branches = (query_rows, out_grad, key_rows, value_rows, skip_gain[None, :])
+    branch_specs = [rows_spec] * 4 + [vector_spec]
+    layer_out, query_grad = kernel(
+        mixing_kernel, convolved, *branches, grid=grid, in_specs=[single_spec] + branch_specs,
+        out_specs=[rows_spec] * 2, out_shape=[rows_shape] * 2,
+    )
+    key_grad, value_grad, filter_grad, skip_grad = kernel(
+        carried_kernel, back, *branches, after=[layer_out], grid=grid, in_specs=[back_spec] + branch_specs,
+        out_specs=[rows_spec] * 3 + [vector_spec],
+        out_shape=[rows_shape] * 3 + [jax.ShapeDtypeStruct((1, channels), F32)],
+    )
+    return (layer_out, query_grad, key_grad, value_grad, filter_grad, skip_grad[0])
 
 
 def rounded_trig(phase, modulus):
@@ -17,7 +310,7 @@
     return lax.all_to_all(blocks, ("outer", "inner"), split_axis=0, concat_axis=0, tiled=True)
 
 
-def body(query_rows, key_rows, value_rows, out_grad, filter_rows, skip_gain):
+def frequency_body(query_rows, key_rows, value_rows, out_grad, filter_rows, skip_gain):
     devices = lax.axis_size(("outer", "inner"))
     position = lax.axis_index(("outer", "inner"))
     tokens_here = query_rows.shape[0]
@@ -118,6 +411,11 @@
     return (layer_out, query_grad, key_grad, value_grad, filter_grad, skip_sum * factor)
 
 
+def body(*arrays):
+    lanes_full = arrays[0].shape[1] == lax.axis_size(AXES) * LANES
+    return (channel_body if lanes_full else frequency_body)(*arrays)
+
+
 def solution(mesh):
     return jax.shard_map(
         body,

time: 995 us -> 187 us (0.19)
  waiting for transfers between devices: 618 us -> 116 us
  local copies, waits for them, and re-layouts: 145 us -> 5.12 us
  blocking collectives: 91.6 us -> 0 us
  other arithmetic: 62.9 us -> 0 us
  matrix products: 49.2 us -> 0 us
  Pallas kernels: 0 us -> 48.9 us
    all_to_all x4, waiting for transfers between devices: 618 us -> 116 us  [exchange(): return lax.all_to_all(blocks, AXES, split_axis=0, concat_axis=0, tiled=True)]
    another operation x12 -> x0, local copies, waits for them, and re-layouts: 103 us -> none  [the longest x4 71.2 us: body(): section_one = regroup_blocks(jnp.stack(section_one, axis=2))]
    psum x1 -> x0, blocking collectives: 91.6 us -> none  [body(): skip_sum = lax.psum(skip_part, ('outer', 'inner'))]
    another operation x16 -> x0, other arithmetic: 49.5 us -> none  [the longest x1 18 us: body(): jnp.stack(section_three, axis=2)]
    dot_general x7 -> x0, matrix products: 49.2 us -> none  [the longest x2 18 us: body(): jnp.einsum('oisbc,iosjk->jkbc', section_one[:, :, half], table_two, prefe...]
    pallas_call x0 -> x6, Pallas kernels: none -> 48.9 us  [kernel(): return pl.pallas_call(waiting, in_specs=specs, **options)(*arrays, *after)]
    squeeze x3 -> x0, local copies, waits for them, and re-layouts: 17.8 us -> none  [the longest x2 16.8 us: body(): spec_real, spec_imag = (spectra[0], spectra[1])]
    slice x1 -> x0, local copies, waits for them, and re-layouts: 11.2 us -> none  [body(): section_one[:, :, half]]
  transfers between devices with their start and end apart: 4 -> 4, of which waited for: 3 -> 4; matrix products, arithmetic and copies ran while one was open for 0% -> 0% of each run, Pallas kernels for 0% -> 21%
where the time goes in v3:
time: 187 us; the launch traced here: 186 us
  waiting for transfers between devices  116 us (62%)
  Pallas kernels  48.9 us (26%)
  starting transfers between devices  15.4 us (8%)
  local copies, waits for them, and re-layouts  5.12 us (3%)
    all_to_all x4, waiting for transfers between devices, exchange(): return lax.all_to_all(blocks, AXES, split_axis=0, concat_axis=0, tiled=True)  116 us
    pallas_call x6, Pallas kernels, kernel(): return pl.pallas_call(waiting, in_specs=specs, **options)(*arrays, *after)  48.9 us
    all_to_all x4, starting transfers between devices, exchange(): return lax.all_to_all(blocks, AXES, split_axis=0, concat_axis=0, tiled=True)  15.4 us
    unnamed x14, local copies, waits for them, and re-layouts  5.12 us
  transfers between devices with their start and end apart: 4, of which 4 were waited for; matrix products, arithmetic and copies ran while one was open for 0% of the time, Pallas kernels for 21%

profile of v3, /device:TPU:0, one launch (start us, length us, event | category | flops | bytes accessed | tf_op | source)
XLA Modules:
  0.0 185.9 jit_solution(14662822896773284642)
XLA Ops:
  0.6 4.1 %shard_map.145.refs_2_ = bf16[32,256,128]{2,1,0:T(8,128)(2,1)} custom-call(bf16[128,4096]{1,0:T(8,128)(2,1)} %refs_0_.2, bf16[128,4096]{1,0:T(8,128)(2,1)} %refs_3_.5, bf16[128,4096]{1,0:T(8,128)(2,1)} %refs_4_.5), custom_call_target="tpu_custom_call" | custom-call | tf_op jit(solution)/shard_map/pallas_call | solution.py:243
  4.7 7.3 %all-to-all-start = ((bf16[32,256,128]{2,1,0:T(8,128)(2,1)}), bf16[32,256,128]{2,1,0:T(8,128)(2,1)S(1)}, u32[]{:S(2)}, u32[]{:S(2)}) async-start(bf16[32,256,128]{2,1,0:T(8,128)(2,1)} %shard_map.145.refs_2_), calls=%async_computation | async-start | bytes 4194304 | tf_op jit(solution)/shard_map/all_to_all | solution.py:229
  12.0 3.6 %shard_map.148 = bf16[32,128,128]{2,1,0:T(8,128)(2,1)} custom-call(bf16[128,4096]{1,0:T(8,128)(2,1)} %refs_1_.8, bf16[128,4096]{1,0:T(8,128)(2,1)} %refs_2_.6, bf16[32,256,128]{2,1,0:T(8,128)(2,1)} %shard_map.145.refs_2_), custom_call_target="tpu_custom_call" | custom-call | tf_op jit(solution)/shard_map/pallas_call | solution.py:243
  15.7 0.0 copy-start.1
  15.7 46.5 %all-to-all-done.refs_0_.refs_1_ = bf16[32,256,128]{2,1,0:T(8,128)(2,1)S(1)} async-done(((bf16[32,256,128]{2,1,0:T(8,128)(2,1)}), bf16[32,256,128]{2,1,0:T(8,128)(2,1)S(1)}, u32[]{:S(2)}, u32[]{:S(2)}) %all-to-all-start) | async-done | bytes 2097184 | tf_op jit(solution)/shard_map/all_to_all | solution.py:229
  62.1 0.0 copy-start
  62.2 2.7 %all-to-all-start.2 = ((bf16[32,128,128]{2,1,0:T(8,128)(2,1)}), bf16[32,128,128]{2,1,0:T(8,128)(2,1)S(1)}, u32[]{:S(2)}, u32[]{:S(2)}) async-start(bf16[32,128,128]{2,1,0:T(8,128)(2,1)} %shard_map.148), calls=%async_computation.2 | async-start | bytes 2097152 | tf_op jit(solution)/shard_map/all_to_all | solution.py:229
  64.8 0.0 copy-done.1
  64.9 0.0 copy-start.3
  64.9 0.9 copy-done.3
  65.8 14.5 %shard_map.146 = (bf16[32,128,128]{2,1,0:T(8,128)(2,1)S(1)}, f32[33,256,256]{2,1,0:T(8,128)}) custom-call(bf16[32,256,128]{2,1,0:T(8,128)(2,1)S(1)} %all-to-all-done.refs_0_.refs_1_, bf16[16,528,256]{2,1,0:T(8,128)(2,1)} %constant.8.clone.refs_1_.refs_3_, bf16[256,256]{1,0:T(8,128)(2,1)S(1)} %copy-done.3, ...), custom_call_target="tpu_custom_call" | custom-call | tf_op jit(solution)/shard_map/pallas_call | solution.py:243
  80.2 0.0 copy-done
  80.3 0.0 copy-start.2
  80.3 1.0 copy-done.2
  81.2 11.2 %all-to-all-done.2.refs_0_ = bf16[32,128,128]{2,1,0:T(8,128)(2,1)S(1)} async-done(((bf16[32,128,128]{2,1,0:T(8,128)(2,1)}), bf16[32,128,128]{2,1,0:T(8,128)(2,1)S(1)}, u32[]{:S(2)}, u32[]{:S(2)}) %all-to-all-start.2) | async-done | bytes 1048608 | tf_op jit(solution)/shard_map/all_to_all | solution.py:229
  92.4 2.6 %all-to-all-start.1 = ((bf16[32,128,128]{2,1,0:T(8,128)(2,1)}), bf16[32,128,128]{2,1,0:T(8,128)(2,1)S(1)}, u32[]{:S(2)}, u32[]{:S(2)}) async-start(bf16[32,128,128]{2,1,0:T(8,128)(2,1)} %copy-done.2), calls=%async_computation.1 | async-start | bytes 2097152 | tf_op jit(solution)/shard_map/all_to_all | solution.py:229
  95.1 0.0 copy-start.4
  95.1 0.9 copy-done.4
  96.0 16.7 %shard_map.149 = bf16[32,272,128]{2,1,0:T(8,128)(2,1)} custom-call(bf16[32,128,128]{2,1,0:T(8,128)(2,1)S(1)} %all-to-all-done.2.refs_0_, bf16[32,256,128]{2,1,0:T(8,128)(2,1)} %copy-done, f32[33,256,256]{2,1,0:T(8,128)} %get-tuple-element.17.refs_2_, bf16[16,528,256]{2,1,0:T(8,128)(2,1)} %constant.8.clone.refs_1_.refs_3_, bf16[256,256]{1,0:T(8,128)(2,1)S(1)} %copy-done.4, ...), custom_call_target="tpu_custom_call" | custom-call | tf_op jit(solution)/shard_map/pallas_call | solution.py:243
  112.7 10.0 %all-to-all-done.1.refs_0_ = bf16[32,128,128]{2,1,0:T(8,128)(2,1)S(1)} async-done(((bf16[32,128,128]{2,1,0:T(8,128)(2,1)}), bf16[32,128,128]{2,1,0:T(8,128)(2,1)S(1)}, u32[]{:S(2)}, u32[]{:S(2)}) %all-to-all-start.1) | async-done | bytes 1048608 | tf_op jit(solution)/shard_map/all_to_all | solution.py:229
  122.7 0.0 copy-start.6
  122.7 1.0 copy-done.6
  123.6 2.8 %all-to-all-start.3 = ((bf16[32,272,128]{2,1,0:T(8,128)(2,1)}), bf16[32,272,128]{2,1,0:T(8,128)(2,1)S(1)}, u32[]{:S(2)}, u32[]{:S(2)}) async-start(bf16[32,272,128]{2,1,0:T(8,128)(2,1)} %shard_map.149), calls=%async_computation.3 | async-start | bytes 4456448 | tf_op jit(solution)/shard_map/all_to_all | solution.py:229
  126.4 4.8 %shard_map.147 = (bf16[128,4096]{1,0:T(8,128)(2,1)}, bf16[128,4096]{1,0:T(8,128)(2,1)}) custom-call(bf16[32,128,128]{2,1,0:T(8,128)(2,1)} %copy-done.6, bf16[128,4096]{1,0:T(8,128)(2,1)} %refs_1_.8, bf16[128,4096]{1,0:T(8,128)(2,1)} %refs_2_.6, bf16[128,4096]{1,0:T(8,128)(2,1)} %refs_3_.5, bf16[128,4096]{1,0:T(8,128)(2,1)} %refs_4_.5, f32[1,4096]{1,0:T(1,128)} %bitcast.2), custom_call_target="tpu_custom_call" | custom-call | tf_op jit(solution)/shard_map/pallas_call | solution.py:243
  131.2 48.1 %all-to-all-done.3.refs_0_ = bf16[32,272,128]{2,1,0:T(8,128)(2,1)S(1)} async-done(((bf16[32,272,128]{2,1,0:T(8,128)(2,1)}), bf16[32,272,128]{2,1,0:T(8,128)(2,1)S(1)}, u32[]{:S(2)}, u32[]{:S(2)}) %all-to-all-start.3) | async-done | bytes 2228256 | tf_op jit(solution)/shard_map/all_to_all | solution.py:229
  179.3 0.0 copy-start.5
  179.3 1.4 copy-done.5
  180.7 5.2 %shard_map.150 = (bf16[128,4096]{1,0:T(8,128)(2,1)}, bf16[128,4096]{1,0:T(8,128)(2,1)}, bf16[128,4096]{1,0:T(8,128)(2,1)}, f32[1,4096]{1,0:T(1,128)}) custom-call(bf16[32,272,128]{2,1,0:T(8,128)(2,1)} %copy-done.5, bf16[128,4096]{1,0:T(8,128)(2,1)} %refs_1_.8, bf16[128,4096]{1,0:T(8,128)(2,1)} %refs_2_.6, bf16[128,4096]{1,0:T(8,128)(2,1)} %refs_3_.5, ...), custom_call_target="tpu_custom_call" | custom-call | tf_op jit(solution)/shard_map/pallas_call | solution.py:243
Async XLA Ops:
  4.7 57.4 %all-to-all-start = ((bf16[32,256,128]{2,1,0:T(8,128)(2,1)}), bf16[32,256,128]{2,1,0:T(8,128)(2,1)S(1)}, u32[]{:S(2)}, u32[]{:S(2)}) async-start(bf16[32,256,128]{2,1,0:T(8,128)(2,1)} %shard_map.145.refs_2_), calls=%async_computation | async-start | bytes 4194304 | tf_op jit(solution)/shard_map/all_to_all | solution.py:229
  15.7 49.2 %copy-start.1 = (bf16[256,528]{1,0:T(8,128)(2,1)S(1)}, bf16[256,528]{1,0:T(8,128)(2,1)}, u32[]{:S(2)}) copy-start(bf16[256,528]{1,0:T(8,128)(2,1)} %constant.11.clone.refs_4_.refs_6_) | copy-start | bytes 811012
  62.1 18.1 %copy-start = (bf16[32,256,128]{2,1,0:T(8,128)(2,1)}, bf16[32,256,128]{2,1,0:T(8,128)(2,1)S(1)}, u32[]{:S(2)}) copy-start(bf16[32,256,128]{2,1,0:T(8,128)(2,1)S(1)} %all-to-all-done.refs_0_.refs_1_) | copy-start | bytes 6291460
  62.2 30.3 %all-to-all-start.2 = ((bf16[32,128,128]{2,1,0:T(8,128)(2,1)}), bf16[32,128,128]{2,1,0:T(8,128)(2,1)S(1)}, u32[]{:S(2)}, u32[]{:S(2)}) async-start(bf16[32,128,128]{2,1,0:T(8,128)(2,1)} %shard_map.148), calls=%async_computation.2 | async-start | bytes 2097152 | tf_op jit(solution)/shard_map/all_to_all | solution.py:229
  64.9 0.9 copy-start.3
  80.3 1.0 copy-start.2
  92.4 30.2 %all-to-all-start.1 = ((bf16[32,128,128]{2,1,0:T(8,128)(2,1)}), bf16[32,128,128]{2,1,0:T(8,128)(2,1)S(1)}, u32[]{:S(2)}, u32[]{:S(2)}) async-start(bf16[32,128,128]{2,1,0:T(8,128)(2,1)} %copy-done.2), calls=%async_computation.1 | async-start | bytes 2097152 | tf_op jit(solution)/shard_map/all_to_all | solution.py:229
  95.1 0.9 copy-start.4
  122.7 1.0 copy-start.6
  123.6 55.7 %all-to-all-start.3 = ((bf16[32,272,128]{2,1,0:T(8,128)(2,1)}), bf16[32,272,128]{2,1,0:T(8,128)(2,1)S(1)}, u32[]{:S(2)}, u32[]{:S(2)}) async-start(bf16[32,272,128]{2,1,0:T(8,128)(2,1)} %shard_map.149), calls=%async_computation.3 | async-start | bytes 4456448 | tf_op jit(solution)/shard_map/all_to_all | solution.py:229
  179.3 1.4 copy-start.5

commit v4 on v3

--- a/solution.py
+++ b/solution.py
@@ -14,7 +14,8 @@
 AXES = ("outer", "inner")
 LANES = 128
 SUBLANES = 8
-SPARE = 2 * SUBLANES
+GROUPS = 4
+SPARE = SUBLANES
 BF16 = jnp.bfloat16
 F32 = jnp.float32
 
@@ -64,12 +65,32 @@
     return pl.ds(pl.multiple_of(b * size, size), size)
 
 
-def pack_kernel(filter_ref, key_ref, value_ref, out_ref):
-    tokens = filter_ref.shape[0]
-    for d in range(out_ref.shape[0]):
-        cols = pl.ds(d * LANES, LANES)
-        out_ref[d, :tokens, :] = filter_ref[:, cols]
-        out_ref[d, tokens:, :] = product_of(key_ref[:, cols], value_ref[:, cols])
+def pack_kernel(filter_ref, key_ref, value_ref, out_ref, held, made, arrived, left):
+    tokens, groups = filter_ref.shape[0], arrived.shape[1]
+    blocks = out_ref.shape[0] // groups
+    sources = (filter_ref, key_ref, value_ref)
+
+    def copies_in(g):
+        cols = pl.ds(g * blocks * LANES, blocks * LANES)
+        return [pltpu.make_async_copy(ref.at[:, cols], held.at[i, :, cols], arrived.at[i, g]) for i, ref in enumerate(sources)]
+
+    def copy_out(g):
+        some = pl.ds(g * blocks, blocks)
+        return pltpu.make_async_copy(made.at[some], out_ref.at[some], left.at[g])
+
+    for g in range(groups):
+        for copy in copies_in(g):
+            copy.start()
+    for g in range(groups):
+        for copy in copies_in(g):
+            copy.wait()
+        for d in range(g * blocks, (g + 1) * blocks):
+            cols = pl.ds(d * LANES, LANES)
+            made[d, :tokens, :] = held[0, :, cols]
+            made[d, tokens:, :] = product_of(held[1, :, cols], held[2, :, cols])
+        copy_out(g).start()
+    for g in range(groups):
+        copy_out(g).wait()
 
 
 def gate_kernel(query_ref, grad_ref, out_ref):
@@ -204,25 +225,51 @@
 
 
 def mixing_kernel(conv_ref, query_ref, grad_ref, key_ref, value_ref, gain_ref, layer_ref, query_grad_ref):
-    for d in range(conv_ref.shape[0]):
+    blocks = layer_ref.shape[1] // LANES
+    for d in range(blocks):
         cols = pl.ds(d * LANES, LANES)
+        query, grad, gain = query_ref[:, cols].astype(F32), grad_ref[:, cols].astype(F32), gain_ref[:, cols]
         product = product_of(key_ref[:, cols], value_ref[:, cols]).astype(F32)
-        mixing = conv_ref[d].astype(F32) + gain_ref[:, cols] * product
-        layer_ref[:, cols] = (query_ref[:, cols].astype(F32) * mixing).astype(BF16)
-        query_grad_ref[:, cols] = (grad_ref[:, cols].astype(F32) * mixing).astype(BF16)
-
-
-def carried_kernel(back_ref, query_ref, grad_ref, key_ref, value_ref, gain_ref, key_grad_ref, value_grad_ref, filter_grad_ref, skip_ref):
-    tokens = query_ref.shape[0]
-    for d in range(back_ref.shape[0]):
-        cols = pl.ds(d * LANES, LANES)
-        gate = grad_ref[:, cols].astype(F32) * query_ref[:, cols].astype(F32)
-        carried = back_ref[d, :tokens, :].astype(F32) + gain_ref[:, cols] * gate
-        key_grad_ref[:, cols] = (carried * value_ref[:, cols].astype(F32)).astype(BF16)
-        value_grad_ref[:, cols] = (carried * key_ref[:, cols].astype(F32)).astype(BF16)
-        filter_grad_ref[:, cols] = back_ref[d, tokens : 2 * tokens, :]
-        spare = back_ref[d, 2 * tokens :, :].astype(F32)
-        skip_ref[:, cols] = jnp.sum(spare, axis=0, keepdims=True)
+        mixing = conv_ref[pl.program_id(0) * blocks + d].astype(F32) + gain * product
+        layer_ref[:, cols] = (query * mixing).astype(BF16)
+        query_grad_ref[:, cols] = (grad * mixing).astype(BF16)
+
+
+def carried_kernel(back_ref, query_ref, grad_ref, key_ref, value_ref, gain_ref, *refs):
+    *row_refs, skip_ref, back, held, made, arrived, left = refs
+    branches = (query_ref, grad_ref, key_ref, value_ref)
+    tokens, groups = key_ref.shape[0], arrived.shape[1]
+    blocks = back_ref.shape[0] // groups
+
+    def copies_in(g):
+        some, cols = pl.ds(g * blocks, blocks), pl.ds(g * blocks * LANES, blocks * LANES)
+        pairs = [(ref.at[:, cols], held.at[i, :, cols]) for i, ref in enumerate(branches)]
+        pairs.append((back_ref.at[some], back.at[some]))
+        return [pltpu.make_async_copy(a, b, arrived.at[i, g]) for i, (a, b) in enumerate(pairs)]
+
+    def copies_out(g):
+        cols = pl.ds(g * blocks * LANES, blocks * LANES)
+        return [pltpu.make_async_copy(made.at[i, :, cols], ref.at[:, cols], left.at[i, g]) for i, ref in enumerate(row_refs)]
+
+    for g in range(groups):
+        for copy in copies_in(g):
+            copy.start()
+    for g in range(groups):
+        for copy in copies_in(g):
+            copy.wait()
+        for d in range(g * blocks, (g + 1) * blocks):
+            cols = pl.ds(d * LANES, LANES)
+            query, grad, key, value = (held[i, :, cols].astype(F32) for i in range(len(branches)))
+            carried = back[d, :tokens, :].astype(F32) + gain_ref[:, cols] * (grad * query)
+            made[0, :, cols] = (carried * value).astype(BF16)
+            made[1, :, cols] = (carried * key).astype(BF16)
+            made[2, :, cols] = back[d, tokens : 2 * tokens, :]
+            skip_ref[:, cols] = jnp.sum(back[d, 2 * tokens :, :].astype(F32), axis=0, keepdims=True)
+        for copy in copies_out(g):
+            copy.start()
+    for g in range(groups):
+        for copy in copies_out(g):
+            copy.wait()
 
 
 def exchange(blocks):
@@ -257,8 +304,6 @@
     rows_spec = pl.BlockSpec((tokens, blocks * LANES), lambda i: (0, i))
     vector_spec = pl.BlockSpec((1, blocks * LANES), lambda i: (0, i))
     single_spec = pl.BlockSpec((blocks, tokens, LANES), lambda i: (i, 0, 0))
-    double_spec = pl.BlockSpec((blocks, 2 * tokens, LANES), lambda i: (i, 0, 0))
-    back_spec = pl.BlockSpec((blocks, back_rows, LANES), lambda i: (i, 0, 0))
     rows_shape = jax.ShapeDtypeStruct((tokens, channels), BF16)
     single_shape = jax.ShapeDtypeStruct((devices, tokens, LANES), BF16)
     double_shape = jax.ShapeDtypeStruct((devices, 2 * tokens, LANES), BF16)
@@ -266,9 +311,15 @@
     narrow = pltpu.VMEM((planes, 2 * tokens, LANES), F32)
     wide = pltpu.VMEM((planes, 2 * tokens, 2 * LANES), F32)
 
+    in_hbm = pl.BlockSpec(memory_space=pltpu.HBM)
+    groups = math.gcd(devices, GROUPS)
     packed = kernel(
-        pack_kernel, filter_rows, key_rows, value_rows, grid=grid,
-        in_specs=[rows_spec] * 3, out_specs=double_spec, out_shape=double_shape,
+        pack_kernel, filter_rows, key_rows, value_rows, in_specs=[in_hbm] * 3, out_specs=in_hbm,
+        out_shape=double_shape, compiler_params=limit(56),
+        scratch_shapes=[
+            pltpu.VMEM((3, tokens, channels), BF16), pltpu.VMEM((devices, 2 * tokens, LANES), BF16),
+            pltpu.SemaphoreType.DMA((3, groups)), pltpu.SemaphoreType.DMA((groups,)),
+        ],
     )
     gate = kernel(
         gate_kernel, query_rows, out_grad, after=[packed], grid=grid,
@@ -287,16 +338,22 @@
         out_shape=back_shape, scratch_shapes=[narrow, narrow, wide], compiler_params=limit(52),
     )
     back = exchange(back)
-    branches = (query_rows, out_grad, key_rows, value_rows, skip_gain[None, :])
-    branch_specs = [rows_spec] * 4 + [vector_spec]
+    whole = pl.BlockSpec(memory_space=pltpu.VMEM)
+    branches = (query_rows, out_grad, key_rows, value_rows)
+    gain = skip_gain[None, :]
     layer_out, query_grad = kernel(
-        mixing_kernel, convolved, *branches, grid=grid, in_specs=[single_spec] + branch_specs,
-        out_specs=[rows_spec] * 2, out_shape=[rows_shape] * 2,
+        mixing_kernel, convolved, *branches, gain, grid=grid, in_specs=[whole] + [rows_spec] * 4 + [vector_spec],
+        out_specs=[rows_spec] * 2, out_shape=[rows_shape] * 2, compiler_params=limit(24),
     )
     key_grad, value_grad, filter_grad, skip_grad = kernel(
-        carried_kernel, back, *branches, after=[layer_out], grid=grid, in_specs=[back_spec] + branch_specs,
-        out_specs=[rows_spec] * 3 + [vector_spec],
-        out_shape=[rows_shape] * 3 + [jax.ShapeDtypeStruct((1, channels), F32)],
+        carried_kernel, back, *branches, gain, in_specs=[in_hbm] * 5 + [pl.BlockSpec()],
+        out_specs=[in_hbm] * 3 + [pl.BlockSpec()],
+        out_shape=[rows_shape] * 3 + [jax.ShapeDtypeStruct((1, channels), F32)], compiler_params=limit(24),
+        scratch_shapes=[
+            pltpu.VMEM((devices, back_rows, LANES), BF16), pltpu.VMEM((4, tokens, channels), BF16),
+            pltpu.VMEM((3, tokens, channels), BF16),
+            pltpu.SemaphoreType.DMA((5, groups)), pltpu.SemaphoreType.DMA((3, groups)),
+        ],
     )
     return (layer_out, query_grad, key_grad, value_grad, filter_grad, skip_grad[0])
 

time: 187 us -> 183 us (0.979)
  Pallas kernels: 48.9 us -> 45.6 us
    pallas_call x6, Pallas kernels: 48.9 us -> 45.6 us  [kernel(): return pl.pallas_call(waiting, in_specs=specs, **options)(*arrays, *after)]
    unnamed x14 -> x22, local copies, waits for them, and re-layouts: 5.12 us -> 4.34 us
where the time goes in v4:
time: 183 us
  waiting for transfers between devices  115 us (63%)
  Pallas kernels  45.6 us (25%)
  starting transfers between devices  17 us (9%)
  local copies, waits for them, and re-layouts  4.34 us (2%)
    all_to_all x4, waiting for transfers between devices, exchange(): return lax.all_to_all(blocks, AXES, split_axis=0, concat_axis=0, tiled=True)  115 us
    pallas_call x6, Pallas kernels, kernel(): return pl.pallas_call(waiting, in_specs=specs, **options)(*arrays, *after)  45.6 us
    all_to_all x4, starting transfers between devices, exchange(): return lax.all_to_all(blocks, AXES, split_axis=0, concat_axis=0, tiled=True)  17 us
    unnamed x22, local copies, waits for them, and re-layouts  4.34 us
  transfers between devices with their start and end apart: 4, of which 4 were waited for; matrix products, arithmetic and copies ran while one was open for 0% of the time, Pallas kernels for 21%

profile of v4, /device:TPU:0, one launch (start us, length us, event | category | flops | bytes accessed | tf_op | source)
XLA Modules:
  0.0 182.6 jit_solution(11303873825195877757)
XLA Ops:
  0.6 2.9 %shard_map.145.refs_2_ = bf16[32,256,128]{2,1,0:T(8,128)(2,1)} custom-call(bf16[128,4096]{1,0:T(8,128)(2,1)} %refs_0_.2, bf16[128,4096]{1,0:T(8,128)(2,1)} %refs_3_.5, bf16[128,4096]{1,0:T(8,128)(2,1)} %refs_4_.5), custom_call_target="tpu_custom_call" | custom-call | tf_op jit(solution)/shard_map/pallas_call | solution.py:290
  3.5 7.3 %all-to-all-start = ((bf16[32,256,128]{2,1,0:T(8,128)(2,1)}), bf16[32,256,128]{2,1,0:T(8,128)(2,1)S(1)}, u32[]{:S(2)}, u32[]{:S(2)}) async-start(bf16[32,256,128]{2,1,0:T(8,128)(2,1)} %shard_map.145.refs_2_), calls=%async_computation | async-start | bytes 4194304 | tf_op jit(solution)/shard_map/all_to_all | solution.py:276
  10.8 3.6 %shard_map.148 = bf16[32,128,128]{2,1,0:T(8,128)(2,1)} custom-call(bf16[128,4096]{1,0:T(8,128)(2,1)} %refs_1_.8, bf16[128,4096]{1,0:T(8,128)(2,1)} %refs_2_.6, bf16[32,256,128]{2,1,0:T(8,128)(2,1)} %shard_map.145.refs_2_), custom_call_target="tpu_custom_call" | custom-call | tf_op jit(solution)/shard_map/pallas_call | solution.py:290
  14.5 0.0 copy-start.6
  14.5 46.5 %all-to-all-done.refs_0_.refs_1_ = bf16[32,256,128]{2,1,0:T(8,128)(2,1)S(1)} async-done(((bf16[32,256,128]{2,1,0:T(8,128)(2,1)}), bf16[32,256,128]{2,1,0:T(8,128)(2,1)S(1)}, u32[]{:S(2)}, u32[]{:S(2)}) %all-to-all-start) | async-done | bytes 2097184 | tf_op jit(solution)/shard_map/all_to_all | solution.py:276
  60.9 0.0 copy-start
  60.9 2.7 %all-to-all-start.2 = ((bf16[32,128,128]{2,1,0:T(8,128)(2,1)}), bf16[32,128,128]{2,1,0:T(8,128)(2,1)S(1)}, u32[]{:S(2)}, u32[]{:S(2)}) async-start(bf16[32,128,128]{2,1,0:T(8,128)(2,1)} %shard_map.148), calls=%async_computation.2 | async-start | bytes 2097152 | tf_op jit(solution)/shard_map/all_to_all | solution.py:276
  63.6 0.0 copy-done.6
  63.7 0.0 copy-start.8
  63.7 0.9 copy-done.8
  64.6 14.5 %shard_map.146 = (bf16[32,128,128]{2,1,0:T(8,128)(2,1)S(1)}, f32[33,256,256]{2,1,0:T(8,128)}) custom-call(bf16[32,256,128]{2,1,0:T(8,128)(2,1)S(1)} %all-to-all-done.refs_0_.refs_1_, bf16[16,528,256]{2,1,0:T(8,128)(2,1)} %constant.8.clone.refs_1_.refs_3_, bf16[256,256]{1,0:T(8,128)(2,1)S(1)} %copy-done.8, ...), custom_call_target="tpu_custom_call" | custom-call | tf_op jit(solution)/shard_map/pallas_call | solution.py:290
  79.0 0.0 copy-done
  79.0 0.0 copy-start.7
  79.0 1.0 copy-done.7
  80.0 11.2 %all-to-all-done.2.refs_0_ = bf16[32,128,128]{2,1,0:T(8,128)(2,1)S(1)} async-done(((bf16[32,128,128]{2,1,0:T(8,128)(2,1)}), bf16[32,128,128]{2,1,0:T(8,128)(2,1)S(1)}, u32[]{:S(2)}, u32[]{:S(2)}) %all-to-all-start.2) | async-done | bytes 1048608 | tf_op jit(solution)/shard_map/all_to_all | solution.py:276
  91.2 0.0 copy-start.9
  91.2 3.5 %all-to-all-start.1 = ((bf16[32,128,128]{2,1,0:T(8,128)(2,1)}), bf16[32,128,128]{2,1,0:T(8,128)(2,1)}, u32[]{:S(2)}, u32[]{:S(2)}) async-start(bf16[32,128,128]{2,1,0:T(8,128)(2,1)} %copy-done.7), calls=%async_computation.1 | async-start | bytes 2097152 | tf_op jit(solution)/shard_map/all_to_all | solution.py:276
  94.8 0.0 copy-done.9
  94.8 16.7 %shard_map.149 = bf16[32,264,128]{2,1,0:T(8,128)(2,1)} custom-call(bf16[32,128,128]{2,1,0:T(8,128)(2,1)S(1)} %all-to-all-done.2.refs_0_, bf16[32,256,128]{2,1,0:T(8,128)(2,1)} %copy-done, f32[33,256,256]{2,1,0:T(8,128)} %get-tuple-element.17.refs_2_, bf16[16,528,256]{2,1,0:T(8,128)(2,1)} %constant.8.clone.refs_1_.refs_3_, bf16[256,256]{1,0:T(8,128)(2,1)S(1)} %copy-done.9, ...), custom_call_target="tpu_custom_call" | custom-call | tf_op jit(solution)/shard_map/pallas_call | solution.py:290
  111.5 0.0 copy-start.1
  111.5 0.0 copy-start.2
  111.5 0.0 copy-start.3
  111.5 0.0 copy-start.10
  111.5 10.8 %all-to-all-done.1.refs_0_ = bf16[32,128,128]{2,1,0:T(8,128)(2,1)} async-done(((bf16[32,128,128]{2,1,0:T(8,128)(2,1)}), bf16[32,128,128]{2,1,0:T(8,128)(2,1)}, u32[]{:S(2)}, u32[]{:S(2)}) %all-to-all-start.1) | async-done | bytes 1048608 | tf_op jit(solution)/shard_map/all_to_all | solution.py:276
  122.3 3.5 %all-to-all-start.3 = ((bf16[32,264,128]{2,1,0:T(8,128)(2,1)}), bf16[32,264,128]{2,1,0:T(8,128)(2,1)}, u32[]{:S(2)}, u32[]{:S(2)}) async-start(bf16[32,264,128]{2,1,0:T(8,128)(2,1)} %shard_map.149), calls=%async_computation.3 | async-start | bytes 4325376 | tf_op jit(solution)/shard_map/all_to_all | solution.py:276
  125.8 0.0 copy-done.1
  125.8 0.0 copy-done.2
  125.9 0.0 copy-done.3
  125.9 0.0 copy-done.10
  125.9 0.0 copy-start.4
  125.9 1.2 copy-done.4
  127.1 3.8 %shard_map.147 = (bf16[128,4096]{1,0:T(8,128)(2,1)}, bf16[128,4096]{1,0:T(8,128)(2,1)}) custom-call(bf16[32,128,128]{2,1,0:T(8,128)(2,1)} %all-to-all-done.1.refs_0_, bf16[128,4096]{1,0:T(8,128)(2,1)S(1)} %copy-done.3, bf16[128,4096]{1,0:T(8,128)(2,1)S(1)} %copy-done.4, bf16[128,4096]{1,0:T(8,128)(2,1)S(1)} %copy-done.1, bf16[128,4096]{1,0:T(8,128)(2,1)S(1)} %copy-done.2, ...), custom_call_target="tpu_custom_call" | custom-call | tf_op jit(solution)/shard_map/pallas_call | solution.py:290
  130.9 46.5 %all-to-all-done.3.refs_0_ = bf16[32,264,128]{2,1,0:T(8,128)(2,1)} async-done(((bf16[32,264,128]{2,1,0:T(8,128)(2,1)}), bf16[32,264,128]{2,1,0:T(8,128)(2,1)}, u32[]{:S(2)}, u32[]{:S(2)}) %all-to-all-start.3) | async-done | bytes 2162720 | tf_op jit(solution)/shard_map/all_to_all | solution.py:276
  177.3 0.0 copy-start.5
  177.3 1.2 copy-done.5
  178.6 4.1 %shard_map.150 = (bf16[128,4096]{1,0:T(8,128)(2,1)}, bf16[128,4096]{1,0:T(8,128)(2,1)}, bf16[128,4096]{1,0:T(8,128)(2,1)}, f32[1,4096]{1,0:T(1,128)}) custom-call(bf16[32,264,128]{2,1,0:T(8,128)(2,1)} %all-to-all-done.3.refs_0_, bf16[128,4096]{1,0:T(8,128)(2,1)S(1)} %copy-done.3, bf16[128,4096]{1,0:T(8,128)(2,1)S(1)} %copy-done.5, ...), custom_call_target="tpu_custom_call" | custom-call | tf_op jit(solution)/shard_map/pallas_call | solution.py:290
Async XLA Ops:
  3.5 57.4 %all-to-all-start = ((bf16[32,256,128]{2,1,0:T(8,128)(2,1)}), bf16[32,256,128]{2,1,0:T(8,128)(2,1)S(1)}, u32[]{:S(2)}, u32[]{:S(2)}) async-start(bf16[32,256,128]{2,1,0:T(8,128)(2,1)} %shard_map.145.refs_2_), calls=%async_computation | async-start | bytes 4194304 | tf_op jit(solution)/shard_map/all_to_all | solution.py:276
  14.5 49.2 %copy-start.6 = (bf16[256,528]{1,0:T(8,128)(2,1)S(1)}, bf16[256,528]{1,0:T(8,128)(2,1)}, u32[]{:S(2)}) copy-start(bf16[256,528]{1,0:T(8,128)(2,1)} %constant.11.clone.refs_4_.refs_6_) | copy-start | bytes 811012
  60.9 18.1 %copy-start = (bf16[32,256,128]{2,1,0:T(8,128)(2,1)}, bf16[32,256,128]{2,1,0:T(8,128)(2,1)S(1)}, u32[]{:S(2)}) copy-start(bf16[32,256,128]{2,1,0:T(8,128)(2,1)S(1)} %all-to-all-done.refs_0_.refs_1_) | copy-start | bytes 6291460
  60.9 30.3 %all-to-all-start.2 = ((bf16[32,128,128]{2,1,0:T(8,128)(2,1)}), bf16[32,128,128]{2,1,0:T(8,128)(2,1)S(1)}, u32[]{:S(2)}, u32[]{:S(2)}) async-start(bf16[32,128,128]{2,1,0:T(8,128)(2,1)} %shard_map.148), calls=%async_computation.2 | async-start | bytes 2097152 | tf_op jit(solution)/shard_map/all_to_all | solution.py:276
  63.7 0.9 copy-start.8
  79.0 1.0 copy-start.7
  91.2 3.5 %copy-start.9 = (bf16[256,256]{1,0:T(8,128)(2,1)S(1)}, bf16[256,256]{1,0:T(8,128)(2,1)}, u32[]{:S(2)}) copy-start(bf16[256,256]{1,0:T(8,128)(2,1)} %constant.9.clone.refs_2_.refs_4_) | copy-start | bytes 393220
  91.2 31.1 %all-to-all-start.1 = ((bf16[32,128,128]{2,1,0:T(8,128)(2,1)}), bf16[32,128,128]{2,1,0:T(8,128)(2,1)}, u32[]{:S(2)}, u32[]{:S(2)}) async-start(bf16[32,128,128]{2,1,0:T(8,128)(2,1)} %copy-done.7), calls=%async_computation.1 | async-start | bytes 2097152 | tf_op jit(solution)/shard_map/all_to_all | solution.py:276
  111.5 14.4 %copy-start.1 = (bf16[128,4096]{1,0:T(8,128)(2,1)S(1)}, bf16[128,4096]{1,0:T(8,128)(2,1)}, u32[]{:S(2)}) copy-start(bf16[128,4096]{1,0:T(8,128)(2,1)} %refs_3_.5) | copy-start | bytes 3145732
  111.5 14.4 %copy-start.2 = (bf16[128,4096]{1,0:T(8,128)(2,1)S(1)}, bf16[128,4096]{1,0:T(8,128)(2,1)}, u32[]{:S(2)}) copy-start(bf16[128,4096]{1,0:T(8,128)(2,1)} %refs_4_.5) | copy-start | bytes 3145732
  111.5 14.4 %copy-start.3 = (bf16[128,4096]{1,0:T(8,128)(2,1)S(1)}, bf16[128,4096]{1,0:T(8,128)(2,1)}, u32[]{:S(2)}) copy-start(bf16[128,4096]{1,0:T(8,128)(2,1)} %refs_1_.8) | copy-start | bytes 3145732
  111.5 14.4 %copy-start.10 = (f32[4096]{0:T(1024)S(1)}, f32[4096]{0:T(1024)}, u32[]{:S(2)}) copy-start(f32[4096]{0:T(1024)} %param.15) | copy-start | bytes 49156
  122.3 55.0 %all-to-all-start.3 = ((bf16[32,264,128]{2,1,0:T(8,128)(2,1)}), bf16[32,264,128]{2,1,0:T(8,128)(2,1)}, u32[]{:S(2)}, u32[]{:S(2)}) async-start(bf16[32,264,128]{2,1,0:T(8,128)(2,1)} %shard_map.149), calls=%async_computation.3 | async-start | bytes 4325376 | tf_op jit(solution)/shard_map/all_to_all | solution.py:276
  125.9 1.2 copy-start.4
  177.3 1.2 copy-start.5

commit v5 on v4

--- a/solution.py
+++ b/solution.py
@@ -15,7 +15,7 @@
 LANES = 128
 SUBLANES = 8
 GROUPS = 4
-SPARE = SUBLANES
+SPARE = 2 * SUBLANES
 BF16 = jnp.bfloat16
 F32 = jnp.float32
 
@@ -236,33 +236,28 @@
 
 
 def carried_kernel(back_ref, query_ref, grad_ref, key_ref, value_ref, gain_ref, *refs):
-    *row_refs, skip_ref, back, held, made, arrived, left = refs
-    branches = (query_ref, grad_ref, key_ref, value_ref)
-    tokens, groups = key_ref.shape[0], arrived.shape[1]
+    *row_refs, skip_ref, back, made, arrived, left = refs
+    tokens, groups = key_ref.shape[0], arrived.shape[0]
     blocks = back_ref.shape[0] // groups
 
-    def copies_in(g):
-        some, cols = pl.ds(g * blocks, blocks), pl.ds(g * blocks * LANES, blocks * LANES)
-        pairs = [(ref.at[:, cols], held.at[i, :, cols]) for i, ref in enumerate(branches)]
-        pairs.append((back_ref.at[some], back.at[some]))
-        return [pltpu.make_async_copy(a, b, arrived.at[i, g]) for i, (a, b) in enumerate(pairs)]
+    def copy_in(g):
+        some = pl.ds(g * blocks, blocks)
+        return pltpu.make_async_copy(back_ref.at[some], back.at[some], arrived.at[g])
 
     def copies_out(g):
         cols = pl.ds(g * blocks * LANES, blocks * LANES)
         return [pltpu.make_async_copy(made.at[i, :, cols], ref.at[:, cols], left.at[i, g]) for i, ref in enumerate(row_refs)]
 
     for g in range(groups):
-        for copy in copies_in(g):
-            copy.start()
-    for g in range(groups):
-        for copy in copies_in(g):
-            copy.wait()
+        copy_in(g).start()
+    for g in range(groups):
+        copy_in(g).wait()
         for d in range(g * blocks, (g + 1) * blocks):
             cols = pl.ds(d * LANES, LANES)
-            query, grad, key, value = (held[i, :, cols].astype(F32) for i in range(len(branches)))
-            carried = back[d, :tokens, :].astype(F32) + gain_ref[:, cols] * (grad * query)
-            made[0, :, cols] = (carried * value).astype(BF16)
-            made[1, :, cols] = (carried * key).astype(BF16)
+            gate = grad_ref[:, cols].astype(F32) * query_ref[:, cols].astype(F32)
+            carried = back[d, :tokens, :].astype(F32) + gain_ref[:, cols] * gate
+            made[0, :, cols] = (carried * value_ref[:, cols].astype(F32)).astype(BF16)
+            made[1, :, cols] = (carried * key_ref[:, cols].astype(F32)).astype(BF16)
             made[2, :, cols] = back[d, tokens : 2 * tokens, :]
             skip_ref[:, cols] = jnp.sum(back[d, 2 * tokens :, :].astype(F32), axis=0, keepdims=True)
         for copy in copies_out(g):
@@ -346,13 +341,12 @@
         out_specs=[rows_spec] * 2, out_shape=[rows_shape] * 2, compiler_params=limit(24),
     )
     key_grad, value_grad, filter_grad, skip_grad = kernel(
-        carried_kernel, back, *branches, gain, in_specs=[in_hbm] * 5 + [pl.BlockSpec()],
+        carried_kernel, back, *branches, gain, in_specs=[in_hbm] + [whole] * 5,
         out_specs=[in_hbm] * 3 + [pl.BlockSpec()],
         out_shape=[rows_shape] * 3 + [jax.ShapeDtypeStruct((1, channels), F32)], compiler_params=limit(24),
         scratch_shapes=[
-            pltpu.VMEM((devices, back_rows, LANES), BF16), pltpu.VMEM((4, tokens, channels), BF16),
-            pltpu.VMEM((3, tokens, channels), BF16),
-            pltpu.SemaphoreType.DMA((5, groups)), pltpu.SemaphoreType.DMA((3, groups)),
+            pltpu.VMEM((devices, back_rows, LANES), BF16), pltpu.VMEM((3, tokens, channels), BF16),
+            pltpu.SemaphoreType.DMA((groups,)), pltpu.SemaphoreType.DMA((3, groups)),
         ],
     )
     return (layer_out, query_grad, key_grad, value_grad, filter_grad, skip_grad[0])

time: 183 us -> 184 us (level)
  no operation moved by 1% of the time
where the time goes in v5:
time: 184 us
  waiting for transfers between devices  116 us (63%)
  Pallas kernels  45.2 us (25%)
  starting transfers between devices  16.9 us (9%)
  local copies, waits for them, and re-layouts  5.24 us (3%)
    all_to_all x4, waiting for transfers between devices, exchange(): return lax.all_to_all(blocks, AXES, split_axis=0, concat_axis=0, tiled=True)  116 us
    pallas_call x6, Pallas kernels, kernel(): return pl.pallas_call(waiting, in_specs=specs, **options)(*arrays, *after)  45.2 us
    all_to_all x4, starting transfers between devices, exchange(): return lax.all_to_all(blocks, AXES, split_axis=0, concat_axis=0, tiled=True)  16.9 us
    unnamed x22, local copies, waits for them, and re-layouts  5.24 us
  transfers between devices with their start and end apart: 4, of which 4 were waited for; matrix products, arithmetic and copies ran while one was open for 0% of the time, Pallas kernels for 21%

profile of v5, /device:TPU:0, one launch (start us, length us, event | category | flops | bytes accessed | tf_op | source)
XLA Modules:
  0.0 183.5 jit_solution(12639678849081748204)
XLA Ops:
  0.6 2.9 %shard_map.145.refs_2_ = bf16[32,256,128]{2,1,0:T(8,128)(2,1)} custom-call(bf16[128,4096]{1,0:T(8,128)(2,1)} %refs_0_.2, bf16[128,4096]{1,0:T(8,128)(2,1)} %refs_3_.5, bf16[128,4096]{1,0:T(8,128)(2,1)} %refs_4_.5), custom_call_target="tpu_custom_call" | custom-call | tf_op jit(solution)/shard_map/pallas_call | solution.py:285
  3.5 7.3 %all-to-all-start = ((bf16[32,256,128]{2,1,0:T(8,128)(2,1)}), bf16[32,256,128]{2,1,0:T(8,128)(2,1)S(1)}, u32[]{:S(2)}, u32[]{:S(2)}) async-start(bf16[32,256,128]{2,1,0:T(8,128)(2,1)} %shard_map.145.refs_2_), calls=%async_computation | async-start | bytes 4194304 | tf_op jit(solution)/shard_map/all_to_all | solution.py:271
  10.8 3.6 %shard_map.148 = bf16[32,128,128]{2,1,0:T(8,128)(2,1)} custom-call(bf16[128,4096]{1,0:T(8,128)(2,1)} %refs_1_.8, bf16[128,4096]{1,0:T(8,128)(2,1)} %refs_2_.6, bf16[32,256,128]{2,1,0:T(8,128)(2,1)} %shard_map.145.refs_2_), custom_call_target="tpu_custom_call" | custom-call | tf_op jit(solution)/shard_map/pallas_call | solution.py:285
  14.5 0.0 copy-start.6
  14.5 46.5 %all-to-all-done.refs_0_.refs_1_ = bf16[32,256,128]{2,1,0:T(8,128)(2,1)S(1)} async-done(((bf16[32,256,128]{2,1,0:T(8,128)(2,1)}), bf16[32,256,128]{2,1,0:T(8,128)(2,1)S(1)}, u32[]{:S(2)}, u32[]{:S(2)}) %all-to-all-start) | async-done | bytes 2097184 | tf_op jit(solution)/shard_map/all_to_all | solution.py:271
  60.9 0.0 copy-start
  60.9 2.7 %all-to-all-start.2 = ((bf16[32,128,128]{2,1,0:T(8,128)(2,1)}), bf16[32,128,128]{2,1,0:T(8,128)(2,1)S(1)}, u32[]{:S(2)}, u32[]{:S(2)}) async-start(bf16[32,128,128]{2,1,0:T(8,128)(2,1)} %shard_map.148), calls=%async_computation.2 | async-start | bytes 2097152 | tf_op jit(solution)/shard_map/all_to_all | solution.py:271
  63.6 0.0 copy-done.6
  63.7 0.0 copy-start.8
  63.7 0.9 copy-done.8
  64.6 14.5 %shard_map.146 = (bf16[32,128,128]{2,1,0:T(8,128)(2,1)S(1)}, f32[33,256,256]{2,1,0:T(8,128)}) custom-call(bf16[32,256,128]{2,1,0:T(8,128)(2,1)S(1)} %all-to-all-done.refs_0_.refs_1_, bf16[16,528,256]{2,1,0:T(8,128)(2,1)} %constant.8.clone.refs_1_.refs_3_, bf16[256,256]{1,0:T(8,128)(2,1)S(1)} %copy-done.8, ...), custom_call_target="tpu_custom_call" | custom-call | tf_op jit(solution)/shard_map/pallas_call | solution.py:285
  79.0 0.0 copy-done
  79.0 0.0 copy-start.7
  79.0 1.0 copy-done.7
  80.0 11.2 %all-to-all-done.2.refs_0_ = bf16[32,128,128]{2,1,0:T(8,128)(2,1)S(1)} async-done(((bf16[32,128,128]{2,1,0:T(8,128)(2,1)}), bf16[32,128,128]{2,1,0:T(8,128)(2,1)S(1)}, u32[]{:S(2)}, u32[]{:S(2)}) %all-to-all-start.2) | async-done | bytes 1048608 | tf_op jit(solution)/shard_map/all_to_all | solution.py:271
  91.2 3.4 %all-to-all-start.1 = ((bf16[32,128,128]{2,1,0:T(8,128)(2,1)}), bf16[32,128,128]{2,1,0:T(8,128)(2,1)}, u32[]{:S(2)}, u32[]{:S(2)}) async-start(bf16[32,128,128]{2,1,0:T(8,128)(2,1)} %copy-done.7), calls=%async_computation.1 | async-start | bytes 2097152 | tf_op jit(solution)/shard_map/all_to_all | solution.py:271
  94.6 0.0 copy-start.9
  94.6 0.9 copy-done.9
  95.5 16.7 %shard_map.149 = bf16[32,272,128]{2,1,0:T(8,128)(2,1)} custom-call(bf16[32,128,128]{2,1,0:T(8,128)(2,1)S(1)} %all-to-all-done.2.refs_0_, bf16[32,256,128]{2,1,0:T(8,128)(2,1)} %copy-done, f32[33,256,256]{2,1,0:T(8,128)} %get-tuple-element.17.refs_2_, bf16[16,528,256]{2,1,0:T(8,128)(2,1)} %constant.8.clone.refs_1_.refs_3_, bf16[256,256]{1,0:T(8,128)(2,1)S(1)} %copy-done.9, ...), custom_call_target="tpu_custom_call" | custom-call | tf_op jit(solution)/shard_map/pallas_call | solution.py:285
  112.2 0.0 copy-start.1
  112.2 0.0 copy-start.2
  112.2 0.0 copy-start.3
  112.2 0.0 copy-start.10
  112.2 10.0 %all-to-all-done.1.refs_0_ = bf16[32,128,128]{2,1,0:T(8,128)(2,1)} async-done(((bf16[32,128,128]{2,1,0:T(8,128)(2,1)}), bf16[32,128,128]{2,1,0:T(8,128)(2,1)}, u32[]{:S(2)}, u32[]{:S(2)}) %all-to-all-start.1) | async-done | bytes 1048608 | tf_op jit(solution)/shard_map/all_to_all | solution.py:271
  122.2 3.5 %all-to-all-start.3 = ((bf16[32,272,128]{2,1,0:T(8,128)(2,1)}), bf16[32,272,128]{2,1,0:T(8,128)(2,1)}, u32[]{:S(2)}, u32[]{:S(2)}) async-start(bf16[32,272,128]{2,1,0:T(8,128)(2,1)} %shard_map.149), calls=%async_computation.3 | async-start | bytes 4456448 | tf_op jit(solution)/shard_map/all_to_all | solution.py:271
  125.7 0.0 copy-done.1
  125.7 0.0 copy-done.2
  125.7 0.0 copy-done.3
  125.7 0.0 copy-done.10
  125.7 0.0 copy-start.4
  125.8 1.2 copy-done.4
  127.0 3.8 %shard_map.147 = (bf16[128,4096]{1,0:T(8,128)(2,1)}, bf16[128,4096]{1,0:T(8,128)(2,1)}) custom-call(bf16[32,128,128]{2,1,0:T(8,128)(2,1)} %all-to-all-done.1.refs_0_, bf16[128,4096]{1,0:T(8,128)(2,1)S(1)} %copy-done.3, bf16[128,4096]{1,0:T(8,128)(2,1)S(1)} %copy-done.4, bf16[128,4096]{1,0:T(8,128)(2,1)S(1)} %copy-done.1, bf16[128,4096]{1,0:T(8,128)(2,1)S(1)} %copy-done.2, ...), custom_call_target="tpu_custom_call" | custom-call | tf_op jit(solution)/shard_map/pallas_call | solution.py:285
  130.7 47.9 %all-to-all-done.3.refs_0_ = bf16[32,272,128]{2,1,0:T(8,128)(2,1)} async-done(((bf16[32,272,128]{2,1,0:T(8,128)(2,1)}), bf16[32,272,128]{2,1,0:T(8,128)(2,1)}, u32[]{:S(2)}, u32[]{:S(2)}) %all-to-all-start.3) | async-done | bytes 2228256 | tf_op jit(solution)/shard_map/all_to_all | solution.py:271
  178.6 0.0 copy-start.5
  178.6 1.2 copy-done.5
  179.8 3.7 %shard_map.150 = (bf16[128,4096]{1,0:T(8,128)(2,1)}, bf16[128,4096]{1,0:T(8,128)(2,1)}, bf16[128,4096]{1,0:T(8,128)(2,1)}, f32[1,4096]{1,0:T(1,128)}) custom-call(bf16[32,272,128]{2,1,0:T(8,128)(2,1)} %all-to-all-done.3.refs_0_, bf16[128,4096]{1,0:T(8,128)(2,1)S(1)} %copy-done.3, bf16[128,4096]{1,0:T(8,128)(2,1)S(1)} %copy-done.5, ...), custom_call_target="tpu_custom_call" | custom-call | tf_op jit(solution)/shard_map/pallas_call | solution.py:285
Async XLA Ops:
  3.5 57.4 %all-to-all-start = ((bf16[32,256,128]{2,1,0:T(8,128)(2,1)}), bf16[32,256,128]{2,1,0:T(8,128)(2,1)S(1)}, u32[]{:S(2)}, u32[]{:S(2)}) async-start(bf16[32,256,128]{2,1,0:T(8,128)(2,1)} %shard_map.145.refs_2_), calls=%async_computation | async-start | bytes 4194304 | tf_op jit(solution)/shard_map/all_to_all | solution.py:271
  14.5 49.2 %copy-start.6 = (bf16[256,528]{1,0:T(8,128)(2,1)S(1)}, bf16[256,528]{1,0:T(8,128)(2,1)}, u32[]{:S(2)}) copy-start(bf16[256,528]{1,0:T(8,128)(2,1)} %constant.11.clone.refs_4_.refs_6_) | copy-start | bytes 811012
  60.9 18.1 %copy-start = (bf16[32,256,128]{2,1,0:T(8,128)(2,1)}, bf16[32,256,128]{2,1,0:T(8,128)(2,1)S(1)}, u32[]{:S(2)}) copy-start(bf16[32,256,128]{2,1,0:T(8,128)(2,1)S(1)} %all-to-all-done.refs_0_.refs_1_) | copy-start | bytes 6291460
  60.9 30.3 %all-to-all-start.2 = ((bf16[32,128,128]{2,1,0:T(8,128)(2,1)}), bf16[32,128,128]{2,1,0:T(8,128)(2,1)S(1)}, u32[]{:S(2)}, u32[]{:S(2)}) async-start(bf16[32,128,128]{2,1,0:T(8,128)(2,1)} %shard_map.148), calls=%async_computation.2 | async-start | bytes 2097152 | tf_op jit(solution)/shard_map/all_to_all | solution.py:271
  63.7 0.9 copy-start.8
  79.0 1.0 copy-start.7
  91.2 31.0 %all-to-all-start.1 = ((bf16[32,128,128]{2,1,0:T(8,128)(2,1)}), bf16[32,128,128]{2,1,0:T(8,128)(2,1)}, u32[]{:S(2)}, u32[]{:S(2)}) async-start(bf16[32,128,128]{2,1,0:T(8,128)(2,1)} %copy-done.7), calls=%async_computation.1 | async-start | bytes 2097152 | tf_op jit(solution)/shard_map/all_to_all | solution.py:271
  94.6 0.9 copy-start.9
  112.2 13.5 %copy-start.1 = (bf16[128,4096]{1,0:T(8,128)(2,1)S(1)}, bf16[128,4096]{1,0:T(8,128)(2,1)}, u32[]{:S(2)}) copy-start(bf16[128,4096]{1,0:T(8,128)(2,1)} %refs_3_.5) | copy-start | bytes 3145732
  112.2 13.5 %copy-start.2 = (bf16[128,4096]{1,0:T(8,128)(2,1)S(1)}, bf16[128,4096]{1,0:T(8,128)(2,1)}, u32[]{:S(2)}) copy-start(bf16[128,4096]{1,0:T(8,128)(2,1)} %refs_4_.5) | copy-start | bytes 3145732
  112.2 13.5 %copy-start.3 = (bf16[128,4096]{1,0:T(8,128)(2,1)S(1)}, bf16[128,4096]{1,0:T(8,128)(2,1)}, u32[]{:S(2)}) copy-start(bf16[128,4096]{1,0:T(8,128)(2,1)} %refs_1_.8) | copy-start | bytes 3145732
  112.2 13.5 %copy-start.10 = (f32[4096]{0:T(1024)S(1)}, f32[4096]{0:T(1024)}, u32[]{:S(2)}) copy-start(f32[4096]{0:T(1024)} %param.15) | copy-start | bytes 49156
  122.2 56.4 %all-to-all-start.3 = ((bf16[32,272,128]{2,1,0:T(8,128)(2,1)}), bf16[32,272,128]{2,1,0:T(8,128)(2,1)}, u32[]{:S(2)}, u32[]{:S(2)}) async-start(bf16[32,272,128]{2,1,0:T(8,128)(2,1)} %shard_map.149), calls=%async_computation.3 | async-start | bytes 4456448 | tf_op jit(solution)/shard_map/all_to_all | solution.py:271
  125.7 1.2 copy-start.4
  178.6 1.2 copy-start.5

commit v6 on v5

--- a/solution.py
+++ b/solution.py
@@ -15,7 +15,7 @@
 LANES = 128
 SUBLANES = 8
 GROUPS = 4
-SPARE = 2 * SUBLANES
+SPARE = SUBLANES
 BF16 = jnp.bfloat16
 F32 = jnp.float32
 

time: 184 us -> 183 us (level)
  no operation moved by 1% of the time
where the time goes in v6:
time: 183 us; the launch traced here: 182 us
  waiting for transfers between devices  115 us (63%)
  Pallas kernels  45.2 us (25%)
  starting transfers between devices  17 us (9%)
  local copies, waits for them, and re-layouts  4.34 us (2%)
    all_to_all x4, waiting for transfers between devices, exchange(): return lax.all_to_all(blocks, AXES, split_axis=0, concat_axis=0, tiled=True)  115 us
    pallas_call x6, Pallas kernels, kernel(): return pl.pallas_call(waiting, in_specs=specs, **options)(*arrays, *after)  45.2 us
    all_to_all x4, starting transfers between devices, exchange(): return lax.all_to_all(blocks, AXES, split_axis=0, concat_axis=0, tiled=True)  17 us
    unnamed x22, local copies, waits for them, and re-layouts  4.34 us
  transfers between devices with their start and end apart: 4, of which 4 were waited for; matrix products, arithmetic and copies ran while one was open for 0% of the time, Pallas kernels for 21%

profile of v6, /device:TPU:0, one launch (start us, length us, event | category | flops | bytes accessed | tf_op | source)
XLA Modules:
  0.0 182.3 jit_solution(5847849172241866233)
XLA Ops:
  0.6 2.9 %shard_map.145.refs_2_ = bf16[32,256,128]{2,1,0:T(8,128)(2,1)} custom-call(bf16[128,4096]{1,0:T(8,128)(2,1)} %refs_0_.2, bf16[128,4096]{1,0:T(8,128)(2,1)} %refs_3_.5, bf16[128,4096]{1,0:T(8,128)(2,1)} %refs_4_.5), custom_call_target="tpu_custom_call" | custom-call | tf_op jit(solution)/shard_map/pallas_call | solution.py:285
  3.5 7.3 %all-to-all-start = ((bf16[32,256,128]{2,1,0:T(8,128)(2,1)}), bf16[32,256,128]{2,1,0:T(8,128)(2,1)S(1)}, u32[]{:S(2)}, u32[]{:S(2)}) async-start(bf16[32,256,128]{2,1,0:T(8,128)(2,1)} %shard_map.145.refs_2_), calls=%async_computation | async-start | bytes 4194304 | tf_op jit(solution)/shard_map/all_to_all | solution.py:271
  10.8 3.6 %shard_map.148 = bf16[32,128,128]{2,1,0:T(8,128)(2,1)} custom-call(bf16[128,4096]{1,0:T(8,128)(2,1)} %refs_1_.8, bf16[128,4096]{1,0:T(8,128)(2,1)} %refs_2_.6, bf16[32,256,128]{2,1,0:T(8,128)(2,1)} %shard_map.145.refs_2_), custom_call_target="tpu_custom_call" | custom-call | tf_op jit(solution)/shard_map/pallas_call | solution.py:285
  14.5 0.0 copy-start.6
  14.5 46.5 %all-to-all-done.refs_0_.refs_1_ = bf16[32,256,128]{2,1,0:T(8,128)(2,1)S(1)} async-done(((bf16[32,256,128]{2,1,0:T(8,128)(2,1)}), bf16[32,256,128]{2,1,0:T(8,128)(2,1)S(1)}, u32[]{:S(2)}, u32[]{:S(2)}) %all-to-all-start) | async-done | bytes 2097184 | tf_op jit(solution)/shard_map/all_to_all | solution.py:271
  60.9 0.0 copy-start
  60.9 2.7 %all-to-all-start.2 = ((bf16[32,128,128]{2,1,0:T(8,128)(2,1)}), bf16[32,128,128]{2,1,0:T(8,128)(2,1)S(1)}, u32[]{:S(2)}, u32[]{:S(2)}) async-start(bf16[32,128,128]{2,1,0:T(8,128)(2,1)} %shard_map.148), calls=%async_computation.2 | async-start | bytes 2097152 | tf_op jit(solution)/shard_map/all_to_all | solution.py:271
  63.6 0.0 copy-done.6
  63.7 0.0 copy-start.8
  63.7 0.9 copy-done.8
  64.6 14.5 %shard_map.146 = (bf16[32,128,128]{2,1,0:T(8,128)(2,1)S(1)}, f32[33,256,256]{2,1,0:T(8,128)}) custom-call(bf16[32,256,128]{2,1,0:T(8,128)(2,1)S(1)} %all-to-all-done.refs_0_.refs_1_, bf16[16,528,256]{2,1,0:T(8,128)(2,1)} %constant.8.clone.refs_1_.refs_3_, bf16[256,256]{1,0:T(8,128)(2,1)S(1)} %copy-done.8, ...), custom_call_target="tpu_custom_call" | custom-call | tf_op jit(solution)/shard_map/pallas_call | solution.py:285
  79.0 0.0 copy-done
  79.0 0.0 copy-start.7
  79.0 1.0 copy-done.7
  80.0 11.2 %all-to-all-done.2.refs_0_ = bf16[32,128,128]{2,1,0:T(8,128)(2,1)S(1)} async-done(((bf16[32,128,128]{2,1,0:T(8,128)(2,1)}), bf16[32,128,128]{2,1,0:T(8,128)(2,1)S(1)}, u32[]{:S(2)}, u32[]{:S(2)}) %all-to-all-start.2) | async-done | bytes 1048608 | tf_op jit(solution)/shard_map/all_to_all | solution.py:271
  91.2 0.0 copy-start.9
  91.2 3.5 %all-to-all-start.1 = ((bf16[32,128,128]{2,1,0:T(8,128)(2,1)}), bf16[32,128,128]{2,1,0:T(8,128)(2,1)}, u32[]{:S(2)}, u32[]{:S(2)}) async-start(bf16[32,128,128]{2,1,0:T(8,128)(2,1)} %copy-done.7), calls=%async_computation.1 | async-start | bytes 2097152 | tf_op jit(solution)/shard_map/all_to_all | solution.py:271
  94.8 0.0 copy-done.9
  94.8 16.7 %shard_map.149 = bf16[32,264,128]{2,1,0:T(8,128)(2,1)} custom-call(bf16[32,128,128]{2,1,0:T(8,128)(2,1)S(1)} %all-to-all-done.2.refs_0_, bf16[32,256,128]{2,1,0:T(8,128)(2,1)} %copy-done, f32[33,256,256]{2,1,0:T(8,128)} %get-tuple-element.17.refs_2_, bf16[16,528,256]{2,1,0:T(8,128)(2,1)} %constant.8.clone.refs_1_.refs_3_, bf16[256,256]{1,0:T(8,128)(2,1)S(1)} %copy-done.9, ...), custom_call_target="tpu_custom_call" | custom-call | tf_op jit(solution)/shard_map/pallas_call | solution.py:285
  111.5 0.0 copy-start.1
  111.5 0.0 copy-start.2
  111.5 0.0 copy-start.3
  111.5 0.0 copy-start.10
  111.5 10.8 %all-to-all-done.1.refs_0_ = bf16[32,128,128]{2,1,0:T(8,128)(2,1)} async-done(((bf16[32,128,128]{2,1,0:T(8,128)(2,1)}), bf16[32,128,128]{2,1,0:T(8,128)(2,1)}, u32[]{:S(2)}, u32[]{:S(2)}) %all-to-all-start.1) | async-done | bytes 1048608 | tf_op jit(solution)/shard_map/all_to_all | solution.py:271
  122.3 3.5 %all-to-all-start.3 = ((bf16[32,264,128]{2,1,0:T(8,128)(2,1)}), bf16[32,264,128]{2,1,0:T(8,128)(2,1)}, u32[]{:S(2)}, u32[]{:S(2)}) async-start(bf16[32,264,128]{2,1,0:T(8,128)(2,1)} %shard_map.149), calls=%async_computation.3 | async-start | bytes 4325376 | tf_op jit(solution)/shard_map/all_to_all | solution.py:271
  125.8 0.0 copy-done.1
  125.8 0.0 copy-done.2
  125.9 0.0 copy-done.3
  125.9 0.0 copy-done.10
  125.9 0.0 copy-start.4
  125.9 1.2 copy-done.4
  127.1 3.8 %shard_map.147 = (bf16[128,4096]{1,0:T(8,128)(2,1)}, bf16[128,4096]{1,0:T(8,128)(2,1)}) custom-call(bf16[32,128,128]{2,1,0:T(8,128)(2,1)} %all-to-all-done.1.refs_0_, bf16[128,4096]{1,0:T(8,128)(2,1)S(1)} %copy-done.3, bf16[128,4096]{1,0:T(8,128)(2,1)S(1)} %copy-done.4, bf16[128,4096]{1,0:T(8,128)(2,1)S(1)} %copy-done.1, bf16[128,4096]{1,0:T(8,128)(2,1)S(1)} %copy-done.2, ...), custom_call_target="tpu_custom_call" | custom-call | tf_op jit(solution)/shard_map/pallas_call | solution.py:285
  130.9 46.5 %all-to-all-done.3.refs_0_ = bf16[32,264,128]{2,1,0:T(8,128)(2,1)} async-done(((bf16[32,264,128]{2,1,0:T(8,128)(2,1)}), bf16[32,264,128]{2,1,0:T(8,128)(2,1)}, u32[]{:S(2)}, u32[]{:S(2)}) %all-to-all-start.3) | async-done | bytes 2162720 | tf_op jit(solution)/shard_map/all_to_all | solution.py:271
  177.3 0.0 copy-start.5
  177.3 1.2 copy-done.5
  178.6 3.7 %shard_map.150 = (bf16[128,4096]{1,0:T(8,128)(2,1)}, bf16[128,4096]{1,0:T(8,128)(2,1)}, bf16[128,4096]{1,0:T(8,128)(2,1)}, f32[1,4096]{1,0:T(1,128)}) custom-call(bf16[32,264,128]{2,1,0:T(8,128)(2,1)} %all-to-all-done.3.refs_0_, bf16[128,4096]{1,0:T(8,128)(2,1)S(1)} %copy-done.3, bf16[128,4096]{1,0:T(8,128)(2,1)S(1)} %copy-done.5, ...), custom_call_target="tpu_custom_call" | custom-call | tf_op jit(solution)/shard_map/pallas_call | solution.py:285
Async XLA Ops:
  3.5 57.4 %all-to-all-start = ((bf16[32,256,128]{2,1,0:T(8,128)(2,1)}), bf16[32,256,128]{2,1,0:T(8,128)(2,1)S(1)}, u32[]{:S(2)}, u32[]{:S(2)}) async-start(bf16[32,256,128]{2,1,0:T(8,128)(2,1)} %shard_map.145.refs_2_), calls=%async_computation | async-start | bytes 4194304 | tf_op jit(solution)/shard_map/all_to_all | solution.py:271
  14.5 49.2 %copy-start.6 = (bf16[256,528]{1,0:T(8,128)(2,1)S(1)}, bf16[256,528]{1,0:T(8,128)(2,1)}, u32[]{:S(2)}) copy-start(bf16[256,528]{1,0:T(8,128)(2,1)} %constant.11.clone.refs_4_.refs_6_) | copy-start | bytes 811012
  60.9 18.1 %copy-start = (bf16[32,256,128]{2,1,0:T(8,128)(2,1)}, bf16[32,256,128]{2,1,0:T(8,128)(2,1)S(1)}, u32[]{:S(2)}) copy-start(bf16[32,256,128]{2,1,0:T(8,128)(2,1)S(1)} %all-to-all-done.refs_0_.refs_1_) | copy-start | bytes 6291460
  60.9 30.3 %all-to-all-start.2 = ((bf16[32,128,128]{2,1,0:T(8,128)(2,1)}), bf16[32,128,128]{2,1,0:T(8,128)(2,1)S(1)}, u32[]{:S(2)}, u32[]{:S(2)}) async-start(bf16[32,128,128]{2,1,0:T(8,128)(2,1)} %shard_map.148), calls=%async_computation.2 | async-start | bytes 2097152 | tf_op jit(solution)/shard_map/all_to_all | solution.py:271
  63.7 0.9 copy-start.8
  79.0 1.0 copy-start.7
  91.2 3.5 %copy-start.9 = (bf16[256,256]{1,0:T(8,128)(2,1)S(1)}, bf16[256,256]{1,0:T(8,128)(2,1)}, u32[]{:S(2)}) copy-start(bf16[256,256]{1,0:T(8,128)(2,1)} %constant.9.clone.refs_2_.refs_4_) | copy-start | bytes 393220
  91.2 31.1 %all-to-all-start.1 = ((bf16[32,128,128]{2,1,0:T(8,128)(2,1)}), bf16[32,128,128]{2,1,0:T(8,128)(2,1)}, u32[]{:S(2)}, u32[]{:S(2)}) async-start(bf16[32,128,128]{2,1,0:T(8,128)(2,1)} %copy-done.7), calls=%async_computation.1 | async-start | bytes 2097152 | tf_op jit(solution)/shard_map/all_to_all | solution.py:271
  111.5 14.4 %copy-start.1 = (bf16[128,4096]{1,0:T(8,128)(2,1)S(1)}, bf16[128,4096]{1,0:T(8,128)(2,1)}, u32[]{:S(2)}) copy-start(bf16[128,4096]{1,0:T(8,128)(2,1)} %refs_3_.5) | copy-start | bytes 3145732
  111.5 14.4 %copy-start.2 = (bf16[128,4096]{1,0:T(8,128)(2,1)S(1)}, bf16[128,4096]{1,0:T(8,128)(2,1)}, u32[]{:S(2)}) copy-start(bf16[128,4096]{1,0:T(8,128)(2,1)} %refs_4_.5) | copy-start | bytes 3145732
  111.5 14.4 %copy-start.3 = (bf16[128,4096]{1,0:T(8,128)(2,1)S(1)}, bf16[128,4096]{1,0:T(8,128)(2,1)}, u32[]{:S(2)}) copy-start(bf16[128,4096]{1,0:T(8,128)(2,1)} %refs_1_.8) | copy-start | bytes 3145732
  111.5 14.4 %copy-start.10 = (f32[4096]{0:T(1024)S(1)}, f32[4096]{0:T(1024)}, u32[]{:S(2)}) copy-start(f32[4096]{0:T(1024)} %param.15) | copy-start | bytes 49156
  122.3 55.0 %all-to-all-start.3 = ((bf16[32,264,128]{2,1,0:T(8,128)(2,1)}), bf16[32,264,128]{2,1,0:T(8,128)(2,1)}, u32[]{:S(2)}, u32[]{:S(2)}) async-start(bf16[32,264,128]{2,1,0:T(8,128)(2,1)} %shard_map.149), calls=%async_computation.3 | async-start | bytes 4325376 | tf_op jit(solution)/shard_map/all_to_all | solution.py:271
  125.9 1.2 copy-start.4
  177.3 1.2 copy-start.5
